TPU v7x, 128 devices: a whole 4x4x4 slice. The times are simulated.
128 devices in a mesh: ctx: 32 (over y, x, core), fsdp: 4 (over z).
Axes of the slice: x: 4, y: 4, z: 4, core: 2. Of those that a mesh axis runs over, the one named last changes fastest.
Arguments:
- tokens: bfloat16 [4, 4096, 960], P('fsdp', 'ctx'), may hold values from -6 to 6
- cotangent: bfloat16 [4, 4096, 960], P('fsdp', 'ctx'), may hold values from -6 to 6
- slot_blocks: int32 [64], replicated, may hold values from 0 to 63, as said below
- norm_gains: bfloat16 [1920], P('fsdp'), may hold values from 0.5 to 1.5
- w_query: bfloat16 [960, 960], P('fsdp'), may hold values from -0.1875 to 0.1875
- w_key: bfloat16 [960, 320], P('fsdp'), may hold values from -0.1875 to 0.1875
- w_value: bfloat16 [960, 320], P('fsdp'), may hold values from -0.1875 to 0.1875
- w_output: bfloat16 [960, 960], P('fsdp'), may hold values from -3.5 to 3.5
- w_gate: bfloat16 [960, 2560], P('fsdp'), may hold values from -0.1875 to 0.1875
- w_up: bfloat16 [960, 2560], P('fsdp'), may hold values from -0.1875 to 0.1875
- w_down: bfloat16 [2560, 960], P('fsdp'), may hold values from -0.125 to 0.125
Outputs:
- layer_out: bfloat16 [4, 4096, 960], P('fsdp', 'ctx')
- input_grad: float32 [4, 4096, 960], P('fsdp', 'ctx')
- grad_gains: float32 [1920], P(('ctx', 'fsdp'))
- grad_query: float32 [960, 960], P('fsdp', 'ctx')
- grad_key: float32 [960, 320], P('fsdp', 'ctx')
- grad_value: float32 [960, 320], P('fsdp', 'ctx')
- grad_output: float32 [960, 960], P('fsdp', 'ctx')
- grad_gate: float32 [960, 2560], P('fsdp', 'ctx')
- grad_up: float32 [960, 2560], P('fsdp', 'ctx')
- grad_down: float32 [2560, 960], P('fsdp', 'ctx')
Inputs may be any that keep to these rules, and one draw needn't show every extreme that they name: `slot_blocks`: A permutation of the 64 blocks of a sequence; entries 2c and 2c + 1 sum to 63.
All inputs are finite; a program needn't handle non-finite values.
Results may differ from a plain program's by a relative error of at most 0.035.
Values may be sent and summed in bfloat16 or wider, within the bound.
A program may use at most 192 MiB of HBM per device.

v0:
```python
import math

import jax
import jax.numpy as jnp
from jax import lax
from jax.sharding import PartitionSpec as P

HEADS = 15
KV_HEADS = 5
HEAD_DIM = 64


epsilon = 1e-05


def multiply(left, right):
    return jnp.dot(left, right, preferred_element_type=jnp.float32)


def multiply_transposed(left, right):
    return lax.dot_general(
        left, right, (((1,), (1,)), ((), ())), preferred_element_type=jnp.float32
    )


def contract_rows(left, right):
    return lax.dot_general(
        left, right, (((0,), (0,)), ((), ())), preferred_element_type=jnp.float32
    )


def rope_tables(positions, head_dim):
    counter = jnp.arange(head_dim // 2, dtype=jnp.float32)
    frequency = jnp.exp(counter * (-2.0 * math.log(10000.0) / head_dim))
    angles = positions.astype(jnp.float32)[:, None] * frequency[None, :]
    return (jnp.cos(angles), jnp.sin(angles))


def rotate(values, cosine, sine):
    half_dim = values.shape[-1] // 2
    first_half = values[..., :half_dim]
    second_half = values[..., half_dim:]
    cos_rows = cosine[:, None, :]
    sin_rows = sine[:, None, :]
    return jnp.concatenate(
        [
            first_half * cos_rows - second_half * sin_rows,
            second_half * cos_rows + first_half * sin_rows,
        ],
        axis=-1,
    )


def unrotate(values, cosine, sine):
    half_dim = values.shape[-1] // 2
    first_half = values[..., :half_dim]
    second_half = values[..., half_dim:]
    cos_rows = cosine[:, None, :]
    sin_rows = sine[:, None, :]
    return jnp.concatenate(
        [
            first_half * cos_rows + second_half * sin_rows,
            second_half * cos_rows - first_half * sin_rows,
        ],
        axis=-1,
    )


def norm_backward(grad_normed, values, inverse_root, gain):
    gain_grad = jnp.sum(grad_normed * values * inverse_root, axis=0)
    scaled = grad_normed * gain
    value_grad = inverse_root * scaled - values * inverse_root**3 * jnp.mean(
        scaled * values, axis=-1, keepdims=True
    )
    return (value_grad, gain_grad)


def shards(
    tokens,
    cotangent,
    slot_blocks,
    norm_gains,
    w_query,
    w_key,
    w_value,
    w_output,
    w_gate,
    w_up,
    w_down,
):
    inputs = tokens[0].astype(jnp.float32)
    row_count, model_width = inputs.shape
    block_len = row_count // 2
    ctx_count = lax.axis_size("ctx")
    ctx_index = lax.axis_index("ctx")
    my_blocks = lax.dynamic_slice_in_dim(slot_blocks, 2 * ctx_index, 2)
    offsets = jnp.arange(block_len, dtype=jnp.int32)
    local_pos = (my_blocks[:, None] * block_len + offsets[None, :]).reshape(row_count)
    key_pos = (slot_blocks[:, None] * block_len + offsets[None, :]).reshape(-1)
    group_size = HEADS // KV_HEADS
    kv_width = KV_HEADS * HEAD_DIM
    group_width = group_size * HEAD_DIM
    score_scale = 1.0 / math.sqrt(HEAD_DIM)
    full_query, full_key, full_value, full_output, full_gate, full_up, full_down, full_gains = (
        lax.all_gather(w_query, "fsdp", axis=0, tiled=True),
        lax.all_gather(w_key, "fsdp", axis=0, tiled=True),
        lax.all_gather(w_value, "fsdp", axis=0, tiled=True),
        lax.all_gather(w_output, "fsdp", axis=0, tiled=True),
        lax.all_gather(w_gate, "fsdp", axis=0, tiled=True),
        lax.all_gather(w_up, "fsdp", axis=0, tiled=True),
        lax.all_gather(w_down, "fsdp", axis=0, tiled=True),
        lax.all_gather(norm_gains, "fsdp", axis=0, tiled=True),
    )
    gain_first = full_gains[:model_width].astype(jnp.float32)
    gain_second = full_gains[model_width:].astype(jnp.float32)
    root_first = lax.rsqrt(jnp.mean(inputs * inputs, axis=-1, keepdims=True) + epsilon)
    normed_first = (inputs * root_first * gain_first).astype(jnp.bfloat16)
    query_raw = multiply(normed_first, full_query)
    key_raw = multiply(normed_first, full_key)
    value_raw = multiply(normed_first, full_value)
    cosine, sine = rope_tables(local_pos, HEAD_DIM)
    queries = rotate(query_raw.reshape(row_count, HEADS, HEAD_DIM), cosine, sine).astype(
        jnp.bfloat16
    )
    keys_local = (
        rotate(key_raw.reshape(row_count, KV_HEADS, HEAD_DIM), cosine, sine)
        .reshape(row_count, kv_width)
        .astype(jnp.bfloat16)
    )
    values_local = value_raw.astype(jnp.bfloat16)
    packed = jnp.concatenate([keys_local, values_local], axis=1)[None]
    gathered = lax.all_gather(packed, "ctx", axis=1, tiled=True)[0]
    row_pos = jnp.repeat(local_pos, group_size)
    visible = key_pos[None, :] <= row_pos[:, None]

    def group_scores(head_group):
        query_rows = queries[:, head_group * group_size : (head_group + 1) * group_size, :].reshape(
            row_count * group_size, HEAD_DIM
        )
        key_rows = gathered[:, head_group * HEAD_DIM : (head_group + 1) * HEAD_DIM]
        scores = multiply_transposed(query_rows, key_rows) * score_scale
        return (query_rows, key_rows, jnp.where(visible, scores, -1e30))

    outputs = []
    log_totals = []
    for head_group in range(KV_HEADS):
        query_rows, key_rows, scores = group_scores(head_group)
        row_max = jnp.max(scores, axis=-1, keepdims=True)
        exponent = jnp.exp(scores - row_max)
        row_total = jnp.sum(exponent, axis=-1, keepdims=True)
        attn_probs = (exponent / row_total).astype(jnp.bfloat16)
        value_rows = gathered[
            :, kv_width + head_group * HEAD_DIM : kv_width + (head_group + 1) * HEAD_DIM
        ]
        mixed = multiply(attn_probs, value_rows)
        outputs.append(mixed.reshape(row_count, group_width))
        log_totals.append(row_max + jnp.log(row_total))
    attended = jnp.concatenate(outputs, axis=1).astype(jnp.bfloat16)
    middle = inputs + multiply(attended, full_output)
    root_second = lax.rsqrt(jnp.mean(middle * middle, axis=-1, keepdims=True) + epsilon)
    normed_second = (middle * root_second * gain_second).astype(jnp.bfloat16)
    gate_proj = multiply(normed_second, full_gate)
    up_proj = multiply(normed_second, full_up)
    gate_sigmoid = jax.nn.sigmoid(gate_proj)
    gate_silu = gate_proj * gate_sigmoid
    hidden = (gate_silu * up_proj).astype(jnp.bfloat16)
    result = middle + multiply(hidden, full_down)
    layer_out = result.astype(jnp.bfloat16)[None]
    back_query, back_key, back_value, back_output, back_gate, back_up, back_down, back_gains = (
        lax.all_gather(w_query, "fsdp", axis=0, tiled=True),
        lax.all_gather(w_key, "fsdp", axis=0, tiled=True),
        lax.all_gather(w_value, "fsdp", axis=0, tiled=True),
        lax.all_gather(w_output, "fsdp", axis=0, tiled=True),
        lax.all_gather(w_gate, "fsdp", axis=0, tiled=True),
        lax.all_gather(w_up, "fsdp", axis=0, tiled=True),
        lax.all_gather(w_down, "fsdp", axis=0, tiled=True),
        lax.all_gather(norm_gains, "fsdp", axis=0, tiled=True),
    )
    back_first = back_gains[:model_width].astype(jnp.float32)
    back_second = back_gains[model_width:].astype(jnp.float32)
    upstream = cotangent[0].astype(jnp.float32)
    upstream_low = upstream.astype(jnp.bfloat16)
    grad_down = contract_rows(hidden, upstream_low)
    grad_hidden = multiply_transposed(upstream_low, back_down)
    grad_gate_proj = (
        grad_hidden * up_proj * gate_sigmoid * (1.0 + gate_proj * (1.0 - gate_sigmoid))
    ).astype(jnp.bfloat16)
    grad_up_proj = (grad_hidden * gate_silu).astype(jnp.bfloat16)
    grad_gate = contract_rows(normed_second, grad_gate_proj)
    grad_up = contract_rows(normed_second, grad_up_proj)
    grad_normed_second = multiply_transposed(grad_gate_proj, back_gate) + multiply_transposed(
        grad_up_proj, back_up
    )
    norm_part, gain_grad_second = norm_backward(
        grad_normed_second, middle, root_second, back_second
    )
    grad_middle = upstream + norm_part
    middle_low = grad_middle.astype(jnp.bfloat16)
    grad_output = contract_rows(attended, middle_low)
    grad_attended = multiply_transposed(middle_low, back_output).astype(jnp.bfloat16)
    query_grads = []
    key_grads = []
    value_grads = []
    for head_group in range(KV_HEADS):
        query_rows, key_rows, scores = group_scores(head_group)
        attn_probs = jnp.exp(scores - log_totals[head_group])
        probs_low = attn_probs.astype(jnp.bfloat16)
        value_rows = gathered[
            :, kv_width + head_group * HEAD_DIM : kv_width + (head_group + 1) * HEAD_DIM
        ]
        grad_rows = grad_attended[
            :, head_group * group_width : (head_group + 1) * group_width
        ].reshape(row_count * group_size, HEAD_DIM)
        value_grads.append(contract_rows(probs_low, grad_rows))
        grad_probs = multiply_transposed(grad_rows, value_rows)
        grad_scores = (
            attn_probs * (grad_probs - jnp.sum(attn_probs * grad_probs, axis=-1, keepdims=True))
        ).astype(jnp.bfloat16)
        query_grads.append(
            (multiply(grad_scores, key_rows) * score_scale).reshape(row_count, group_width)
        )
        key_grads.append(contract_rows(grad_scores, query_rows) * score_scale)
    kv_partial = jnp.concatenate(key_grads + value_grads, axis=1)[None]
    kv_summed = lax.psum_scatter(
        kv_partial.astype(jnp.bfloat16), "ctx", scatter_dimension=1, tiled=True
    ).astype(jnp.float32)[0]
    grad_query_raw = (
        unrotate(
            jnp.concatenate(query_grads, axis=1).reshape(row_count, HEADS, HEAD_DIM), cosine, sine
        )
        .reshape(row_count, model_width)
        .astype(jnp.bfloat16)
    )
    grad_key_raw = (
        unrotate(kv_summed[:, :kv_width].reshape(row_count, KV_HEADS, HEAD_DIM), cosine, sine)
        .reshape(row_count, kv_width)
        .astype(jnp.bfloat16)
    )
    grad_value_low = kv_summed[:, kv_width:].astype(jnp.bfloat16)
    grad_query = contract_rows(normed_first, grad_query_raw)
    grad_key = contract_rows(normed_first, grad_key_raw)
    grad_value = contract_rows(normed_first, grad_value_low)
    grad_normed_first = (
        multiply_transposed(grad_query_raw, back_query)
        + multiply_transposed(grad_key_raw, back_key)
        + multiply_transposed(grad_value_low, back_value)
    )
    norm_first_part, gain_grad_first = norm_backward(
        grad_normed_first, inputs, root_first, back_first
    )
    input_grad = grad_middle + norm_first_part
    gain_grid = jnp.concatenate([gain_grad_first, gain_grad_second]).reshape(ctx_count, -1)
    part_query, part_key, part_value, part_output, part_gate, part_up, part_down, part_gains = (
        lax.psum_scatter(
            grad_query.astype(jnp.bfloat16), "ctx", scatter_dimension=1, tiled=True
        ).astype(jnp.float32),
        lax.psum_scatter(
            grad_key.astype(jnp.bfloat16), "ctx", scatter_dimension=1, tiled=True
        ).astype(jnp.float32),
        lax.psum_scatter(
            grad_value.astype(jnp.bfloat16), "ctx", scatter_dimension=1, tiled=True
        ).astype(jnp.float32),
        lax.psum_scatter(
            grad_output.astype(jnp.bfloat16), "ctx", scatter_dimension=1, tiled=True
        ).astype(jnp.float32),
        lax.psum_scatter(
            grad_gate.astype(jnp.bfloat16), "ctx", scatter_dimension=1, tiled=True
        ).astype(jnp.float32),
        lax.psum_scatter(
            grad_up.astype(jnp.bfloat16), "ctx", scatter_dimension=1, tiled=True
        ).astype(jnp.float32),
        lax.psum_scatter(
            grad_down.astype(jnp.bfloat16), "ctx", scatter_dimension=1, tiled=True
        ).astype(jnp.float32),
        lax.psum_scatter(
            gain_grid.astype(jnp.bfloat16), "ctx", scatter_dimension=0, tiled=True
        ).astype(jnp.float32),
    )
    sum_query, sum_key, sum_value, sum_output, sum_gate, sum_up, sum_down, sum_gains = (
        lax.psum_scatter(
            part_query.astype(jnp.bfloat16), "fsdp", scatter_dimension=0, tiled=True
        ).astype(jnp.float32),
        lax.psum_scatter(
            part_key.astype(jnp.bfloat16), "fsdp", scatter_dimension=0, tiled=True
        ).astype(jnp.float32),
        lax.psum_scatter(
            part_value.astype(jnp.bfloat16), "fsdp", scatter_dimension=0, tiled=True
        ).astype(jnp.float32),
        lax.psum_scatter(
            part_output.astype(jnp.bfloat16), "fsdp", scatter_dimension=0, tiled=True
        ).astype(jnp.float32),
        lax.psum_scatter(
            part_gate.astype(jnp.bfloat16), "fsdp", scatter_dimension=0, tiled=True
        ).astype(jnp.float32),
        lax.psum_scatter(
            part_up.astype(jnp.bfloat16), "fsdp", scatter_dimension=0, tiled=True
        ).astype(jnp.float32),
        lax.psum_scatter(
            part_down.astype(jnp.bfloat16), "fsdp", scatter_dimension=0, tiled=True
        ).astype(jnp.float32),
        lax.psum_scatter(
            part_gains.astype(jnp.bfloat16), "fsdp", scatter_dimension=1, tiled=True
        ).astype(jnp.float32),
    )
    return (
        layer_out,
        input_grad[None],
        sum_gains.reshape(-1),
        sum_query,
        sum_key,
        sum_value,
        sum_output,
        sum_gate,
        sum_up,
        sum_down,
    )


def solution(mesh):
    return jax.shard_map(
        shards,
        mesh=mesh,
        in_specs=(
            P("fsdp", "ctx", None),
            P("fsdp", "ctx", None),
            P(),
            P("fsdp"),
            P("fsdp", None),
            P("fsdp", None),
            P("fsdp", None),
            P("fsdp", None),
            P("fsdp", None),
            P("fsdp", None),
            P("fsdp", None),
        ),
        out_specs=(
            P("fsdp", "ctx", None),
            P("fsdp", "ctx", None),
            P(("ctx", "fsdp")),
            P("fsdp", "ctx"),
            P("fsdp", "ctx"),
            P("fsdp", "ctx"),
            P("fsdp", "ctx"),
            P("fsdp", "ctx"),
            P("fsdp", "ctx"),
            P("fsdp", "ctx"),
        ),
        check_vma=False,
    )
```

profile of v0, /device:TPU:0, one launch (start us, length us, event | category | flops | bytes accessed | tf_op | source)
XLA Modules:
  0.0 911.6 jit_solution(6937429081595250817)
XLA Ops:
  8.9 15.1 %all-gather.1 = bf16[4,240,320]{1,2,0:T(8,128)(2,1)S(1)} all-gather(bf16[1,240,320]{1,2,0:T(8,128)(2,1)} %bitcast.230), channel_id=1, replica_groups=mesh['ctx'=32,'fsdp'=4] {'fsdp'}, dimensions={0}, use_global_device_ids=true | all-gather | bytes 768000 | tf_op jit(solution)/shard_map/all_gather | solution.py:106
  25.1 17.7 %all-gather.2 = bf16[4,240,320]{1,2,0:T(8,128)(2,1)S(1)} all-gather(bf16[1,240,320]{1,2,0:T(8,128)(2,1)} %bitcast.231), channel_id=1, replica_groups=mesh['ctx'=32,'fsdp'=4] {'fsdp'}, dimensions={0}, use_global_device_ids=true | all-gather | bytes 768000 | tf_op jit(solution)/shard_map/all_gather | solution.py:107
  45.5 10.1 %all-reduce = bf16[1920]{0:T(1024)(128)(2,1)S(1)} all-reduce(bf16[1920]{0:T(1024)(128)(2,1)S(1)} %dynamic-update-slice), channel_id=1, replica_groups=mesh['ctx'=32,'fsdp'=4] {'fsdp'}, use_global_device_ids=true, to_apply=%add | all-reduce | flops 1920 | bytes 7680
  66.5 42.9 %all-gather.20.cloned.1.call-done = bf16[4096,640]{0,1:T(8,128)(2,1)} async-done(((bf16[128,640]{0,1:T(8,128)(2,1)}), bf16[4096,640]{0,1:T(8,128)(2,1)}) %all-gather.20.cloned.1.call-update) | async-done | bytes 5242896 | tf_op jit(solution)/shard_map/all_gather | solution.py:132
  149.7 46.8 %all-gather.16.cloned.1.call-done = bf16[960,2560]{1,0:T(8,128)(2,1)} async-done(((bf16[240,2560]{1,0:T(8,128)(2,1)}), bf16[960,2560]{1,0:T(8,128)(2,1)}) %all-gather.16.cloned.1.call-update) | async-done | bytes 4915216 | tf_op jit(solution)/shard_map/all_gather | solution.py:110
  200.9 52.0 %all-gather.14.cloned.1.call-done = bf16[960,2560]{1,0:T(8,128)(2,1)} async-done(((bf16[240,2560]{1,0:T(8,128)(2,1)}), bf16[960,2560]{1,0:T(8,128)(2,1)}) %all-gather.14.cloned.1.call-update) | async-done | bytes 4915216 | tf_op jit(solution)/shard_map/all_gather | solution.py:109
  257.2 52.0 %all-gather.18.cloned.1.call-done = bf16[2560,960]{0,1:T(8,128)(2,1)} async-done(((bf16[640,960]{0,1:T(8,128)(2,1)}), bf16[2560,960]{0,1:T(8,128)(2,1)}) %all-gather.18.cloned.1.call-update) | async-done | bytes 4915216 | tf_op jit(solution)/shard_map/all_gather | solution.py:111
  309.2 5.4 multiply_convert_fusion.5
  345.3 5.7 multiply_reduce_fusion.3
  350.9 6.8 multiply_convert_fusion.3
  363.0 6.6 multiply_convert_fusion.2
  374.7 6.8 multiply_convert_fusion.1
  412.3 101.5 %fusion.130 = (bf16[960,32]{0,1:T(8,128)(2,1)}, bf16[960,32]{0,1:T(8,128)(2,1)}, bf16[2560,32]{0,1:T(8,128)(2,1)S(1)}) fusion(bf16[960,960]{0,1:T(8,128)(2,1)} %convolution_convert_fusion.9, bf16[960,960]{0,1:T(8,128)(2,1)} %convolution_convert_fusion.8, bf16[2560,960]{0,1:T(8,128)(2,1)} %convolution_convert_fusion.2), kind=kCustom, calls=%all-reduce-scatter.3 | all-reduce-scatter fusion | flops 4587521 | bytes 8888832
  563.0 21.4 %copy.78 = bf16[1,4096,640]{2,0,1:T(2,128)(2,1)} copy(bf16[1,4096,640]{1,2,0:T(8,128)(2,1)} %fusion.27) | data formatting | bytes 10485760
  584.4 7.2 copy.98
  601.9 6.4 reduce-scatter.52.cloned.1.call-done
  609.9 21.0 %reduce-scatter.50.cloned.1.call-done = bf16[240,80]{1,0:T(8,128)(2,1)} async-done(((bf16[960,80]{1,0:T(8,128)(2,1)}), bf16[240,80]{1,0:T(8,128)(2,1)}) %reduce-scatter.50.cloned.1.call-update) | async-done | bytes 38416
  632.5 21.5 %reduce-scatter.48.cloned.1.call-done = bf16[240,80]{1,0:T(8,128)(2,1)} async-done(((bf16[960,80]{1,0:T(8,128)(2,1)}), bf16[240,80]{1,0:T(8,128)(2,1)}) %reduce-scatter.48.cloned.1.call-update) | async-done | bytes 38416
  655.5 86.2 %reduce-scatter.38.cloned.1.call-done = bf16[128,640]{1,0:T(8,128)(2,1)} async-done(((bf16[4096,640]{1,0:T(8,128)(2,1)}), bf16[128,640]{1,0:T(8,128)(2,1)}) %reduce-scatter.38.cloned.1.call-update) | async-done | bytes 163856
  753.5 64.3 %all-reduce.1 = bf16[32,60]{1,0:T(8,128)(2,1)S(1)} all-reduce(bf16[32,60]{1,0:T(8,128)(2,1)S(1)} %pad_maximum_fusion.3), channel_id=4, replica_groups=mesh['ctx'=32,'fsdp'=4] {'ctx'}, use_global_device_ids=true, to_apply=%region_22.23.clone | all-reduce | flops 1920 | bytes 7680
  818.5 10.7 %all-reduce.2 = bf16[1,60]{1,0:T(2,128)(2,1)S(1)} all-reduce(bf16[1,60]{1,0:T(2,128)(2,1)S(1)} %constant_dynamic-slice_fusion.6), channel_id=5, replica_groups=mesh['ctx'=32,'fsdp'=4] {'fsdp'}, use_global_device_ids=true, to_apply=%region_23.24.clone | all-reduce | flops 60 | bytes 240
  830.8 26.9 %all-reduce.15.cloned.1.call-done = (bf16[960,320]{0,1:T(8,128)(2,1)}, bf16[960,320]{0,1:T(8,128)(2,1)}) async-done(((bf16[960,320]{0,1:T(8,128)(2,1)}, bf16[960,320]{0,1:T(8,128)(2,1)}), (bf16[960,320]{0,1:T(8,128)(2,1)}, bf16[960,320]{0,1:T(8,128)(2,1)})) %all-reduce.15.cloned.1.call-update) | async-done | bytes 1228816
  861.7 18.9 %reduce-scatter.44.cloned.1.call-done = bf16[240,10]{1,0:T(8,128)(2,1)} async-done(((bf16[960,10]{1,0:T(8,128)(2,1)}), bf16[240,10]{1,0:T(8,128)(2,1)}) %reduce-scatter.44.cloned.1.call-update) | async-done | bytes 4816
  882.2 21.2 %reduce-scatter.42.cloned.1.call-done = bf16[240,10]{1,0:T(8,128)(2,1)} async-done(((bf16[960,10]{1,0:T(8,128)(2,1)}), bf16[240,10]{1,0:T(8,128)(2,1)}) %reduce-scatter.42.cloned.1.call-update) | async-done | bytes 4816
  (428 shorter events, 218.4 us)
Async XLA Ops:
  7.2 54.1 %all-gather.10.cloned.1.call-start = ((), (), s32[]{:S(2)}) async-start(), calls=%async_computation.10 | async-start | bytes 2457600 | tf_op jit(solution)/shard_map/all_gather | solution.py:105
  8.0 101.4 %all-gather.20.cloned.1.call-start = ((), (), s32[]{:S(2)}) async-start(), calls=%async_computation.17 | async-start | bytes 5406720 | tf_op jit(solution)/shard_map/all_gather | solution.py:132
  56.4 348.2 %copy-start.74 = (f32[128]{0:T(128)}, f32[128]{0:T(128)S(1)}, u32[]{:S(2)}) copy-start(f32[128]{0:T(128)S(1)} %get-tuple-element.52) | copy-start | bytes 1540
  58.3 88.7 %all-gather.12.cloned.1.call-start = ((), (), s32[]{:S(2)}) async-start(), calls=%async_computation.11 | async-start | bytes 2457600 | tf_op jit(solution)/shard_map/all_gather | solution.py:108
  59.0 137.5 %all-gather.16.cloned.1.call-start = ((), (), s32[]{:S(2)}) async-start(), calls=%async_computation.13 | async-start | bytes 6144000 | tf_op jit(solution)/shard_map/all_gather | solution.py:110
  59.6 193.2 %all-gather.14.cloned.1.call-start = ((), (), s32[]{:S(2)}) async-start(), calls=%async_computation.12 | async-start | bytes 6144000 | tf_op jit(solution)/shard_map/all_gather | solution.py:109
  60.2 249.0 %all-gather.18.cloned.1.call-start = ((), (), s32[]{:S(2)}) async-start(), calls=%async_computation.14 | async-start | bytes 6144000 | tf_op jit(solution)/shard_map/all_gather | solution.py:111
  60.8 488.9 %reduce-scatter.36.cloned.1.call-start = ((), (), s32[]{:S(2)}) async-start(), calls=%async_computation.16 | async-start | bytes 5406720 | tf_op jit(solution)/shard_map/reduce_scatter | solution.py:269
  318.5 237.9 %reduce-scatter.34.cloned.1.call-start = ((), (), s32[]{:S(2)}) async-start(), calls=%async_computation.15 | async-start | bytes 5406720 | tf_op jit(solution)/shard_map/reduce_scatter | solution.py:266
  334.9 263.8 %reduce-scatter.46.cloned.1.call-start = ((), (), s32[]{:S(2)}) async-start(), calls=%async_computation.22 | async-start | bytes 307200
  514.8 18.8 %collective-permute-start.2 = (bf16[960,32]{0,1:T(8,128)(2,1)}, bf16[960,32]{0,1:T(8,128)(2,1)}, u32[]{:S(2)}, u32[]{:S(2)}) collective-permute-start(bf16[960,32]{0,1:T(8,128)(2,1)} %get-tuple-element.20), channel_id=1, source_target_pairs={{0,4},{4,8},{8,12},{12,16},{16,20},{20,24},{24,28},{28,32},{32,36}... | collective-permute-start | bytes 184328
  517.0 15.3 %collective-permute-start.3 = (bf16[960,30]{0,1:T(8,128)(2,1)S(1)}, bf16[960,30]{0,1:T(8,128)(2,1)S(1)}, u32[]{:S(2)}, u32[]{:S(2)}) collective-permute-start(bf16[960,30]{0,1:T(8,128)(2,1)S(1)} %slice.183), channel_id=1, source_target_pairs={{0,8},{4,12},{8,16},{12,20},{16,24},{20,28},{24,32},{28,36},{32,40... | collective-permute-start | bytes 172808
  528.3 13.1 %collective-permute-start = (bf16[960,32]{0,1:T(8,128)(2,1)S(1)}, bf16[960,32]{0,1:T(8,128)(2,1)S(1)}, u32[]{:S(2)}, u32[]{:S(2)}) collective-permute-start(bf16[960,32]{0,1:T(8,128)(2,1)S(1)} %copy-done.45), channel_id=1, source_target_pairs={{0,4},{4,8},{8,12},{12,16},{16,20},{20,24},{24,28},{28,32},{32,36}... | collective-permute-start | bytes 184328
  529.6 13.2 %collective-permute-start.4 = (bf16[2560,32]{0,1:T(8,128)(2,1)S(1)}, bf16[2560,32]{0,1:T(8,128)(2,1)S(1)}, u32[]{:S(2)}, u32[]{:S(2)}) collective-permute-start(bf16[2560,32]{0,1:T(8,128)(2,1)S(1)} %get-tuple-element.21), channel_id=1, source_target_pairs={{0,4},{4,8},{8,12},{12,16},{16,20},{20,24},{24,28},{28,32},{32,36}... | collective-permute-start | bytes 491528
  531.0 10.5 %collective-permute-start.1 = (bf16[960,30]{0,1:T(8,128)(2,1)S(1)}, bf16[960,30]{0,1:T(8,128)(2,1)S(1)}, u32[]{:S(2)}, u32[]{:S(2)}) collective-permute-start(bf16[960,30]{0,1:T(8,128)(2,1)S(1)} %slice.182), channel_id=1, source_target_pairs={{0,8},{4,12},{8,16},{12,20},{16,24},{20,28},{24,32},{28,36},{32,40... | collective-permute-start | bytes 172808
  532.3 10.5 %collective-permute-start.5 = (bf16[2560,30]{0,1:T(8,128)(2,1)S(1)}, bf16[2560,30]{0,1:T(8,128)(2,1)S(1)}, u32[]{:S(2)}, u32[]{:S(2)}) collective-permute-start(bf16[2560,30]{0,1:T(8,128)(2,1)S(1)} %slice.184), channel_id=1, source_target_pairs={{0,8},{4,12},{8,16},{12,20},{16,24},{20,28},{24,32},{28,36},{32,40... | collective-permute-start | bytes 460808
  536.5 63.8 %reduce-scatter.40.cloned.1.call-start = ((), (), s32[]{:S(2)}) async-start(), calls=%async_computation.19 | async-start | bytes 307200
  542.8 65.5 %reduce-scatter.52.cloned.1.call-start = ((), (), s32[]{:S(2)}) async-start(), calls=%async_computation.25 | async-start | bytes 819200
  544.8 86.2 %reduce-scatter.50.cloned.1.call-start = ((), (), s32[]{:S(2)}) async-start(), calls=%async_computation.24 | async-start | bytes 307200
  551.5 102.5 %reduce-scatter.48.cloned.1.call-start = ((), (), s32[]{:S(2)}) async-start(), calls=%async_computation.23 | async-start | bytes 307200
  558.1 183.5 %reduce-scatter.38.cloned.1.call-start = ((), (), s32[]{:S(2)}) async-start(), calls=%async_computation.18 | async-start | bytes 5406720
  591.6 266.1 %all-reduce.15.cloned.1.call-start = ((), (), s32[]{:S(2)}) async-start(), calls=%async_computation.26 | async-start | bytes 2621440
  752.8 127.9 %reduce-scatter.44.cloned.1.call-start = ((), (), s32[]{:S(2)}) async-start(), calls=%async_computation.21 | async-start | bytes 307200
  859.4 44.0 %reduce-scatter.42.cloned.1.call-start = ((), (), s32[]{:S(2)}) async-start(), calls=%async_computation.20 | async-start | bytes 307200
  (89 other events, 3253.3 us)
Sparse Core Ops, SparseCore 0:
  9.7 37.7 all-gather.9
  58.4 50.9 all-gather.19
  111.1 29.5 all-gather.11
  142.2 54.3 all-gather.15
  198.1 54.7 all-gather.13
  254.4 54.7 all-gather.17
  318.6 84.7 reduce-scatter.35
  407.5 90.5 reduce-scatter.33
  536.6 24.6 reduce-scatter.45
  563.6 20.4 reduce-scatter.39
  586.6 21.6 reduce-scatter.51
  610.4 20.4 reduce-scatter.49
  633.4 20.4 reduce-scatter.47
  657.5 84.1 reduce-scatter.37
  752.9 104.6 all-reduce.14
  860.0 20.6 reduce-scatter.43
  882.9 20.4 reduce-scatter.41
where the time goes:
time: 918 us; the launch traced here: 912 us
  waiting for transfers between devices  399 us (43%)
  blocking collectives  219 us (24%)
  matrix products  143 us (16%)
  local copies, waits for them, and re-layouts  79.3 us (9%)
  other arithmetic  43.1 us (5%)
  between operations  18.5 us (2%)
  starting transfers between devices  9.68 us (1%)
    unnamed x32, waiting for transfers between devices  205 us
    unnamed x4, blocking collectives  187 us
    unnamed x219, local copies, waits for them, and re-layouts  67.5 us
    dot_general x17, matrix products, multiply_transposed(): lax.dot_general(left, right, (((1,), (1,)), ((), ())), preferred_element_...  57.2 us
    all_gather x1, waiting for transfers between devices, shards(): lax.all_gather(w_down, 'fsdp', axis=0, tiled=True)  52 us
    all_gather x1, waiting for transfers between devices, shards(): lax.all_gather(w_gate, 'fsdp', axis=0, tiled=True)  52 us
    all_gather x1, waiting for transfers between devices, shards(): lax.all_gather(w_up, 'fsdp', axis=0, tiled=True)  46.8 us
    dot_general x17, matrix products, contract_rows(): lax.dot_general(left, right, (((0,), (0,)), ((), ())), preferred_element_...  45.1 us
  transfers between devices with their start and end apart: 23, of which 11 were waited for; matrix products, arithmetic and copies ran while one was open for 36% of the time, Pallas kernels for 0%

commit v1 on v0

v1 whole, which is shorter than its diff:
```python
import math

import jax
import jax.numpy as jnp
from jax import lax
from jax.experimental import pallas as pl
from jax.experimental.pallas import tpu as pltpu
from jax.sharding import Mesh
from jax.sharding import PartitionSpec as P

HEADS = 15
KV_HEADS = 5
HEAD_DIM = 64
GROUP = HEADS // KV_HEADS
BLK = 64
TILE = 512
PAIR = 2 * HEAD_DIM
LANES = 256
D = 960
FF = 2560
CTX = ("y", "x", "c")
ALL = ("y", "x", "c", "z")
TEAM = ("x", "c")

epsilon = 1e-05
NT = (((1,), (1,)), ((), ()))


def multiply(left, right):
    return jnp.dot(left, right, preferred_element_type=jnp.float32)


def multiply_transposed(left, right):
    return lax.dot_general(left, right, NT, preferred_element_type=jnp.float32)


def contract_rows(left, right):
    return lax.dot_general(
        left, right, (((0,), (0,)), ((), ())), preferred_element_type=jnp.float32
    )


def rope_tables(positions):
    counter = jnp.arange(HEAD_DIM // 2, dtype=jnp.float32)
    frequency = jnp.exp(counter * (-2.0 * math.log(10000.0) / HEAD_DIM))
    angles = positions.astype(jnp.float32)[:, None] * frequency[None, :]
    return (jnp.cos(angles), jnp.sin(angles))


def rotate(values, cosine, sine):
    half = HEAD_DIM // 2
    first, second = values[..., :half], values[..., half:]
    cos_rows, sin_rows = cosine[:, None, :], sine[:, None, :]
    return jnp.concatenate(
        [first * cos_rows - second * sin_rows, second * cos_rows + first * sin_rows], axis=-1
    )


def norm_backward(grad_normed, values, inverse_root, gain):
    gain_grad = jnp.sum(grad_normed * values * inverse_root, axis=0)
    scaled = grad_normed * gain
    value_grad = inverse_root * scaled - values * inverse_root**3 * jnp.mean(
        scaled * values, axis=-1, keepdims=True
    )
    return (value_grad, gain_grad)


def load_by_position(slots_ref, kv_hbm, kv, sem):
    def start(slot, _):
        pltpu.make_async_copy(
            kv_hbm.at[slot], kv.at[pl.ds(slots_ref[slot] * BLK, BLK)], sem
        ).start()
        return 0

    lax.fori_loop(0, 64, start, 0)

    pltpu.make_async_copy(kv, kv, sem).wait()


def pick(offset):
    row = lax.broadcasted_iota(jnp.int32, (HEAD_DIM, PAIR), 0)
    lane = lax.broadcasted_iota(jnp.int32, (HEAD_DIM, PAIR), 1)
    return jnp.where(lane == row + offset, 1.0, 0.0).astype(jnp.bfloat16)


def hidden_keys(block):
    key = lax.broadcasted_iota(jnp.int32, (TILE, LANES), 0)
    lane = lax.broadcasted_iota(jnp.int32, (TILE, LANES), 1)
    return key > lax.rem(lane, BLK) + lax.rem(block, TILE // BLK) * BLK


def forward_kernel(slots_ref, mine_ref, q_ref, kv_hbm, out_ref, lse_ref, kv, acc, top, total, sem):
    load_by_position(slots_ref, kv_hbm, kv, sem)
    value_rows = pick(HEAD_DIM)
    for half in range(2):
        block = mine_ref[half]
        full = lax.div(block, TILE // BLK)
        top[...] = jnp.full_like(top, -1e30)
        total[...] = jnp.zeros_like(total)
        acc[...] = jnp.zeros_like(acc)

        def tile(index, masked):
            rows = pl.ds(pl.multiple_of(index * TILE, TILE), TILE)
            hide = hidden_keys(block) if masked else None
            for g in range(KV_HEADS):
                pair = kv[rows, g * PAIR : (g + 1) * PAIR]
                scores = multiply_transposed(pair, q_ref[half, g])
                if masked:
                    scores = jnp.where(hide, -1e30, scores)
                before = top[g]
                now = jnp.maximum(before, jnp.max(scores, axis=0, keepdims=True))
                weights = jnp.exp(scores - now)
                shrink = jnp.exp(before - now)
                top[g] = now
                total[g] = total[g] * shrink + jnp.sum(weights, axis=0, keepdims=True)
                turned = multiply_transposed(value_rows, pair).astype(jnp.bfloat16)
                acc[g] = acc[g] * shrink + multiply(turned, weights.astype(jnp.bfloat16))

        def step(index, _):
            tile(index, False)
            return 0

        lax.fori_loop(0, full, step, 0)
        tile(full, True)
        for g in range(KV_HEADS):
            out_ref[half, g] = acc[g] / total[g]
            lse_ref[half, g] = top[g] + jnp.log(total[g])


def backward_kernel(
    slots_ref, mine_ref, q_ref, do_ref, out_ref, lse_ref, kv_hbm, dq_ref, dkv_hbm,
    kv, grads, low, delta, acc, sem, out_sem,
):
    load_by_position(slots_ref, kv_hbm, kv, sem)
    grads[...] = jnp.zeros_like(grads)
    key_rows = pick(0)
    value_rows = pick(HEAD_DIM)
    for half in range(2):
        block = mine_ref[half]
        full = lax.div(block, TILE // BLK)
        acc[...] = jnp.zeros_like(acc)
        for g in range(KV_HEADS):
            delta[g] = jnp.sum(
                multiply_transposed(value_rows, do_ref[half, g]) * out_ref[half, g],
                axis=0,
                keepdims=True,
            )

        def tile(index, masked):
            rows = pl.ds(pl.multiple_of(index * TILE, TILE), TILE)
            hide = hidden_keys(block) if masked else None
            for g in range(KV_HEADS):
                pair = kv[rows, g * PAIR : (g + 1) * PAIR]
                scores = multiply_transposed(pair, q_ref[half, g])
                weights = jnp.exp(scores - lse_ref[half, g])
                if masked:
                    weights = jnp.where(hide, 0.0, weights)
                grad_weights = multiply_transposed(pair, do_ref[half, g])
                grad_scores = (weights * (grad_weights - delta[g])).astype(jnp.bfloat16)
                grads[rows, g * PAIR : (g + 1) * PAIR] += multiply(
                    grad_scores, q_ref[half, g]
                ) + multiply(weights.astype(jnp.bfloat16), do_ref[half, g])
                turned = multiply_transposed(key_rows, pair).astype(jnp.bfloat16)
                acc[g] += multiply(turned, grad_scores)

        def step(index, _):
            tile(index, False)
            return 0

        lax.fori_loop(0, full, step, 0)
        tile(full, True)
        dq_ref[half] = acc[...] * 0.125

    def lower(index, _):
        rows = pl.ds(pl.multiple_of(index * TILE, TILE), TILE)
        low[rows, :] = grads[rows, :].astype(jnp.bfloat16)
        return 0

    lax.fori_loop(0, low.shape[0] // TILE, lower, 0)

    def start(slot, _):
        ctx = lax.div(slot, 2)
        y, x, c = lax.div(ctx, 8), lax.rem(lax.div(ctx, 2), 4), lax.rem(ctx, 2)
        place = dkv_hbm.at[c, x * (1 - c) + y * c, y * (1 - c) + x * c]
        pltpu.make_async_copy(
            low.at[pl.ds(slots_ref[slot] * BLK, BLK)],
            place.at[pl.ds(lax.rem(slot, 2) * BLK, BLK)],
            out_sem,
        ).start()
        return 0

    lax.fori_loop(0, 64, start, 0)

    pltpu.make_async_copy(low, low, out_sem).wait()


def attend_forward(slots, mine, queries, gathered):
    smem = pl.BlockSpec(memory_space=pltpu.SMEM)
    vmem = pl.BlockSpec(memory_space=pltpu.VMEM)
    length, width = gathered.shape[0] * BLK, gathered.shape[2]
    return pl.pallas_call(
        forward_kernel,
        out_shape=(
            jax.ShapeDtypeStruct((2, KV_HEADS, HEAD_DIM, LANES), jnp.float32),
            jax.ShapeDtypeStruct((2, KV_HEADS, 1, LANES), jnp.float32),
        ),
        in_specs=[smem, smem, vmem, pl.BlockSpec(memory_space=pl.ANY)],
        out_specs=(vmem, vmem),
        scratch_shapes=[
            pltpu.VMEM((length, width), jnp.bfloat16),
            pltpu.VMEM((KV_HEADS, HEAD_DIM, LANES), jnp.float32),
            pltpu.VMEM((KV_HEADS, 1, LANES), jnp.float32),
            pltpu.VMEM((KV_HEADS, 1, LANES), jnp.float32),
            pltpu.SemaphoreType.DMA,
        ],
        compiler_params=pltpu.CompilerParams(vmem_limit_bytes=48 * 2**20),
        cost_estimate=pl.CostEstimate(
            flops=10_000_000_000, bytes_accessed=8_000_000, transcendentals=5_000_000
        ),
    )(slots, mine, queries, gathered)


def attend_backward(slots, mine, queries, grad_out, out, lse, gathered):
    smem = pl.BlockSpec(memory_space=pltpu.SMEM)
    vmem = pl.BlockSpec(memory_space=pltpu.VMEM)
    hbm = pl.BlockSpec(memory_space=pl.ANY)
    length, width = gathered.shape[0] * BLK, gathered.shape[2]
    return pl.pallas_call(
        backward_kernel,
        out_shape=(
            jax.ShapeDtypeStruct((2, KV_HEADS, HEAD_DIM, LANES), jnp.float32),
            jax.ShapeDtypeStruct((2, 4, 4, 2 * BLK, width), jnp.bfloat16),
        ),
        in_specs=[smem, smem, vmem, vmem, vmem, vmem, hbm],
        out_specs=(vmem, hbm),
        scratch_shapes=[
            pltpu.VMEM((length, width), jnp.bfloat16),
            pltpu.VMEM((length, width), jnp.float32),
            pltpu.VMEM((length, width), jnp.bfloat16),
            pltpu.VMEM((KV_HEADS, 1, LANES), jnp.float32),
            pltpu.VMEM((KV_HEADS, HEAD_DIM, LANES), jnp.float32),
            pltpu.SemaphoreType.DMA,
            pltpu.SemaphoreType.DMA,
        ],
        compiler_params=pltpu.CompilerParams(vmem_limit_bytes=48 * 2**20),
        cost_estimate=pl.CostEstimate(
            flops=20_000_000_000, bytes_accessed=12_000_000, transcendentals=5_000_000
        ),
    )(slots, mine, queries, grad_out, out, lse, gathered)


def by_group(values, before):
    parts = values.reshape(2, BLK, KV_HEADS, GROUP, HEAD_DIM).transpose(0, 2, 3, 1, 4)
    parts = parts.reshape(2, KV_HEADS, GROUP * BLK, HEAD_DIM).astype(jnp.bfloat16)
    return jnp.pad(
        parts,
        ((0, 0), (0, 0), (0, LANES - GROUP * BLK), (before, PAIR - HEAD_DIM - before)),
    )


def from_group(turned):
    parts = turned[..., : GROUP * BLK].reshape(2, KV_HEADS, HEAD_DIM, GROUP, BLK)
    return parts.transpose(0, 4, 1, 3, 2).reshape(2 * BLK, HEADS, HEAD_DIM)


MESH_IDS = pl.DeviceIdType.MESH


def remote(source, target, send_sem, recv_sem, device):
    return pltpu.make_async_remote_copy(
        src_ref=source,
        dst_ref=target,
        send_sem=send_sem,
        recv_sem=recv_sem,
        device_id=device,
        device_id_type=MESH_IDS,
    )


def greet(devices):
    barrier = pltpu.get_barrier_semaphore()
    for device in devices:
        pl.semaphore_signal(barrier, inc=1, device_id=device, device_id_type=MESH_IDS)
    pl.semaphore_wait(barrier, len(devices))


def ffn_kernel(
    h_ref, cot_ref, gate_up_ref, down_ref,
    dh_ref, partial_ref, grads_ref,
    rows, grad, hid, dgate, dup, mine, from_sibling, kept, halves, passed, arrived,
    gather_send, gather_recv, sib_send, sib_recv, ring_send, ring_recv,
):
    x, c = lax.axis_index("x"), lax.axis_index("c")
    right, left, across = lax.rem(x + 1, 4), lax.rem(x + 3, 4), lax.rem(x + 2, 4)
    other = 1 - c
    to_right, to_left, to_sibling = {"x": right}, {"x": left}, {"c": other}
    half = BLK
    top, low = pl.ds(0, half), pl.ds(half, half)
    greet((to_right, to_left, to_sibling))

    rows[x, c] = h_ref[...]
    spot = rows.at[x, c]
    first = [
        remote(spot, spot, gather_send.at[0], gather_recv.at[0], to_right),
        remote(spot, spot, gather_send.at[1], gather_recv.at[1], to_left),
        remote(spot, spot, sib_send.at[0], sib_recv.at[0], to_sibling),
    ]
    for copy in first:
        copy.start()
    from_left, from_right, from_far = rows.at[left, c], rows.at[right, c], rows.at[across, c]
    gate_w, up_w = gate_up_ref[0], gate_up_ref[1]
    down_w = down_ref[...]

    def work(chip, step):
        block = rows[chip].reshape(4 * BLK, D)
        gate = multiply(block, gate_w)
        up = multiply(block, up_w)
        grad_hidden = multiply_transposed(cot_ref[chip].reshape(4 * BLK, D), down_w)
        sigmoid = 1.0 / (1.0 + jnp.exp(-gate))
        silu = gate * sigmoid
        hidden = (silu * up).astype(jnp.bfloat16)
        grad_gate = (grad_hidden * up * sigmoid * (1.0 + gate * (1.0 - sigmoid))).astype(jnp.bfloat16)
        grad_up = (grad_hidden * silu).astype(jnp.bfloat16)
        hid[chip] = hidden
        dgate[chip] = grad_gate
        dup[chip] = grad_up
        grad_rows = multiply_transposed(grad_gate, gate_w) + multiply_transposed(grad_up, up_w)
        kept[step] = grad_rows.reshape(2, 2 * BLK, D)
        mine[step] = kept[step, other].astype(jnp.bfloat16)
        copy = remote(
            mine.at[step], from_sibling.at[step], sib_send.at[4 + step], sib_recv.at[4 + step], to_sibling
        )
        copy.start()
        partial_ref[chip] = multiply(hidden, down_w).astype(jnp.bfloat16).reshape(2, 2 * BLK, D)
        return copy

    first[2].wait_recv()
    backs = [work(x, 0)]
    first[0].wait_recv()
    forward_right = remote(
        from_left.at[top], from_left.at[top], gather_send.at[2], gather_recv.at[2], to_right
    )
    forward_right.start()
    sib_left = remote(from_left, from_left, sib_send.at[1], sib_recv.at[1], to_sibling)
    sib_left.start()
    first[1].wait_recv()
    forward_left = remote(
        from_right.at[low], from_right.at[low], gather_send.at[3], gather_recv.at[3], to_left
    )
    forward_left.start()
    sib_right = remote(from_right, from_right, sib_send.at[2], sib_recv.at[2], to_sibling)
    sib_right.start()
    sib_left.wait_recv()
    backs.append(work(left, 1))
    sib_right.wait_recv()
    backs.append(work(right, 2))
    forward_right.wait_recv()
    forward_left.wait_recv()
    sib_far = remote(from_far, from_far, sib_send.at[3], sib_recv.at[3], to_sibling)
    sib_far.start()
    sib_far.wait_recv()
    backs.append(work(across, 3))

    backs[3].wait_recv()
    far = kept[3, c] + from_sibling[3].astype(jnp.float32)
    halves[...] = far.astype(jnp.bfloat16)
    far_right = remote(halves.at[top], arrived.at[0, top], ring_send.at[0], ring_recv.at[0], to_right)
    far_left = remote(halves.at[low], arrived.at[0, low], ring_send.at[1], ring_recv.at[1], to_left)
    far_right.start()
    far_left.start()
    unit = FF // 32
    slabs = [(z, y) for z in range(4) for y in range(4)]

    def keep(start, down):
        for z, y in slabs:
            line, column = (z, y) if down else (y, z)
            piece = grad[
                line * unit : (line + 1) * unit, column * (D // 4) : (column + 1) * (D // 4)
            ]
            grads_ref[z, y, start : start + unit] = piece.astype(jnp.bfloat16)

    grad[...] = contract_rows(
        dgate[...].reshape(16 * BLK, FF // 8), rows[...].reshape(16 * BLK, D)
    )
    keep(0, False)
    for step in range(3):
        backs[step].wait_recv()
        kept[step, c] += from_sibling[step].astype(jnp.float32)
    far_right.wait_recv()
    passed[0, top] = (kept[2, c, top] + arrived[0, top].astype(jnp.float32)).astype(jnp.bfloat16)
    passed[0, low] = kept[2, c, low].astype(jnp.bfloat16)
    near_right = remote(passed.at[0], arrived.at[1], ring_send.at[2], ring_recv.at[2], to_right)
    near_right.start()
    far_left.wait_recv()
    passed[1, top] = kept[1, c, top].astype(jnp.bfloat16)
    passed[1, low] = (kept[1, c, low] + arrived[0, low].astype(jnp.float32)).astype(jnp.bfloat16)
    near_left = remote(passed.at[1], arrived.at[2], ring_send.at[3], ring_recv.at[3], to_left)
    near_left.start()
    grad[...] = contract_rows(
        dup[...].reshape(16 * BLK, FF // 8), rows[...].reshape(16 * BLK, D)
    )
    keep(unit, False)
    grad[...] = contract_rows(
        hid[...].reshape(16 * BLK, FF // 8), cot_ref[...].reshape(16 * BLK, D)
    )
    keep(2 * unit, True)
    near_right.wait_recv()
    near_left.wait_recv()
    dh_ref[...] = (
        kept[0, c] + arrived[1].astype(jnp.float32) + arrived[2].astype(jnp.float32)
    )
    for copy in first + [forward_right, forward_left, sib_left, sib_right, sib_far]:
        copy.wait_send()
    for copy in backs + [far_right, far_left, near_right, near_left]:
        copy.wait_send()


def feed_forward(normed, team_cotangent, gate_up, down):
    vmem = pl.BlockSpec(memory_space=pltpu.VMEM)
    width = FF // 8
    return pl.pallas_call(
        ffn_kernel,
        out_shape=(
            jax.ShapeDtypeStruct((2 * BLK, D), jnp.float32),
            jax.ShapeDtypeStruct((4, 2, 2 * BLK, D), jnp.bfloat16),
            jax.ShapeDtypeStruct((4, 4, 3 * FF // 32, D // 4), jnp.bfloat16),
        ),
        in_specs=[vmem] * 4,
        out_specs=(vmem,) * 3,
        scratch_shapes=[
            pltpu.VMEM((4, 2, 2 * BLK, D), jnp.bfloat16),
            pltpu.VMEM((width, D), jnp.float32),
            pltpu.VMEM((4, 4 * BLK, width), jnp.bfloat16),
            pltpu.VMEM((4, 4 * BLK, width), jnp.bfloat16),
            pltpu.VMEM((4, 4 * BLK, width), jnp.bfloat16),
            pltpu.VMEM((4, 2 * BLK, D), jnp.bfloat16),
            pltpu.VMEM((4, 2 * BLK, D), jnp.bfloat16),
            pltpu.VMEM((4, 2, 2 * BLK, D), jnp.float32),
            pltpu.VMEM((2 * BLK, D), jnp.bfloat16),
            pltpu.VMEM((2, 2 * BLK, D), jnp.bfloat16),
            pltpu.VMEM((3, 2 * BLK, D), jnp.bfloat16),
            pltpu.SemaphoreType.DMA((4,)),
            pltpu.SemaphoreType.DMA((4,)),
            pltpu.SemaphoreType.DMA((8,)),
            pltpu.SemaphoreType.DMA((8,)),
            pltpu.SemaphoreType.DMA((4,)),
            pltpu.SemaphoreType.DMA((4,)),
        ],
        compiler_params=pltpu.CompilerParams(
            collective_id=1, has_side_effects=True, vmem_limit_bytes=56 * 2**20
        ),
        cost_estimate=pl.CostEstimate(
            flops=6_000_000_000, bytes_accessed=12_000_000, transcendentals=400_000
        ),
    )(normed, team_cotangent, gate_up, down)


def ring_of(axis):
    place = lax.axis_index(axis)
    return place, {axis: lax.rem(place + 1, 4)}, {axis: lax.rem(place + 3, 4)}


def plane_rings():
    x, y, c = lax.axis_index("x"), lax.axis_index("y"), lax.axis_index("c")

    def along(step_x, step_y):
        return {"y": lax.rem(y + step_y, 4), "x": lax.rem(x + step_x, 4)}

    first = (x * (1 - c) + y * c, along(1 - c, c), along(3 * (1 - c), 3 * c))
    second = (y * (1 - c) + x * c, along(c, 1 - c), along(3 * c, 3 * (1 - c)))
    return first, second


def cut(rows):
    top = (rows // 2 + 15) // 16 * 16
    return pl.ds(0, top), pl.ds(top, rows - top)


class RingGather:
    def __init__(self, ring, own, spot, parts, send, recv):
        self.place, self.right, self.left = ring
        self.own, self.spot, self.parts, self.send, self.recv = own, spot, parts, send, recv
        self.begun = []

    def _go(self, source, target, index, device):
        copy = remote(source, target, self.send.at[index], self.recv.at[index], device)
        copy.start()
        self.begun.append(copy)
        return copy

    def near(self):
        target = self.spot(self.place)
        self.to_right = self._go(self.own, target, 0, self.right)
        self.to_left = self._go(self.own, target, 1, self.left)

    def from_left(self):
        self.to_right.wait_recv()
        block = self.spot(lax.rem(self.place + 3, 4))
        piece = block.at[self.parts[0]]
        self.on_right = self._go(piece, piece, 2, self.right)
        return block

    def from_right(self):
        self.to_left.wait_recv()
        block = self.spot(lax.rem(self.place + 1, 4))
        piece = block.at[self.parts[1]]
        self.on_left = self._go(piece, piece, 3, self.left)
        return block

    def from_far(self):
        self.on_right.wait_recv()
        self.on_left.wait_recv()
        return self.spot(lax.rem(self.place + 2, 4))

    def drain(self):
        for copy in self.begun:
            copy.wait_send()


class Passing:
    def __init__(self, send, recv):
        self.send, self.recv, self.copies = send, recv, []
        self.device = {"c": 1 - lax.axis_index("c")}

    def go(self, source, target):
        k = len(self.copies)
        copy = remote(source, target, self.send.at[k], self.recv.at[k], self.device)
        copy.start()
        self.copies.append(copy)

    def wait(self):
        for copy in self.copies:
            copy.wait_recv()

    def drain(self):
        for copy in self.copies:
            copy.wait_send()


def first_gather_kernel(
    w_ref, gain_ref, w_out, gain_out,
    w_send, w_recv, gain_send, gain_recv, sib_send, sib_recv, local,
):
    c = lax.axis_index("c")
    z_ring = ring_of("z")
    greet((z_ring[1], z_ring[2], {"c": 1 - c}))
    passing = Passing(sib_send, sib_recv)
    weights = RingGather(
        z_ring, w_ref.at[c], lambda i: w_out.at[c, i], cut(w_ref.shape[1]), w_send, w_recv
    )
    gains = RingGather(
        z_ring, gain_ref, lambda i: gain_out.at[i], cut(gain_ref.shape[0]), gain_send, gain_recv
    )
    weights.near()
    gains.near()
    z = z_ring[0]
    own = [
        pltpu.make_async_copy(w_ref, w_out.at[:, z], local.at[0]),
        pltpu.make_async_copy(gain_ref, gain_out.at[z], local.at[1]),
    ]
    for copy in own:
        copy.start()
    for turn in ("from_left", "from_right", "from_far"):
        block = getattr(weights, turn)()
        passing.go(block, block)
        getattr(gains, turn)()
    passing.wait()
    for copy in own:
        copy.wait()
    weights.drain()
    gains.drain()
    passing.drain()


def second_gather_kernel(
    kv_ref, o_ref, down_ref, kv_out, o_out, down_out,
    kv_send, kv_recv, o_send, o_recv, down_send, down_recv, sib_send, sib_recv, o_sib_send, o_sib_recv, local,
):
    x, y, c = lax.axis_index("x"), lax.axis_index("y"), lax.axis_index("c")
    z_ring = ring_of("z")
    first, second = plane_rings()
    greet((first[1], first[2], second[1], second[2], z_ring[1], z_ring[2], {"c": 1 - c}))
    a0 = first[0]

    def spot(a, b):
        return kv_out.at[b * (1 - c) + a * c, a * (1 - c) + b * c, c]

    rows = cut(kv_ref.shape[0])
    passing = Passing(sib_send, sib_recv)
    o_passing = Passing(o_sib_send, o_sib_recv)

    def hand(block):
        passing.go(block, block)

    stage = RingGather(
        first, kv_ref, lambda a: spot(a, second[0]), rows, kv_send.at[0], kv_recv.at[0]
    )

    def spread_ring(k, shift, own):
        a = lax.rem(a0 + shift, 4)
        ring = RingGather(
            second, own, lambda b: spot(a, b), rows, kv_send.at[1 + k], kv_recv.at[1 + k]
        )
        ring.near()
        return ring

    stage.near()
    ring_own = spread_ring(0, 0, kv_ref)
    passing.go(kv_ref, spot(a0, second[0]))
    z_rings = (
        RingGather(z_ring, o_ref.at[c], lambda i: o_out.at[c, i], cut(o_ref.shape[1]), o_send, o_recv),
        RingGather(z_ring, down_ref, lambda i: down_out.at[i], cut(down_ref.shape[0]), down_send, down_recv),
    )
    for ring in z_rings:
        ring.near()
    z = z_ring[0]
    own = [
        pltpu.make_async_copy(kv_ref, kv_out.at[y, x, c], local.at[0]),
        pltpu.make_async_copy(o_ref, o_out.at[:, z], local.at[1]),
        pltpu.make_async_copy(down_ref, down_out.at[z], local.at[2]),
    ]
    for copy in own:
        copy.start()
    block = stage.from_left()
    ring_left = spread_ring(1, 3, block)
    hand(block)
    block = stage.from_right()
    ring_right = spread_ring(2, 1, block)
    hand(block)
    block = stage.from_far()
    ring_far = spread_ring(3, 2, block)
    hand(block)
    plane = (ring_own, ring_left, ring_right, ring_far)
    for turn in ("from_left", "from_right"):
        for ring in plane:
            hand(getattr(ring, turn)())
        block = getattr(z_rings[0], turn)()
        o_passing.go(block, block)
        getattr(z_rings[1], turn)()
    for ring in plane:
        hand(ring.from_far())
    block = z_rings[0].from_far()
    o_passing.go(block, block)
    z_rings[1].from_far()
    passing.wait()
    o_passing.wait()
    for copy in own:
        copy.wait()
    for ring in (stage,) + plane + z_rings:
        ring.drain()
    passing.drain()
    o_passing.drain()


def dma(*counts):
    return [pltpu.SemaphoreType.DMA(n if isinstance(n, tuple) else (n,)) for n in counts]


def first_gather(weights, gains):
    hbm = pl.BlockSpec(memory_space=pl.ANY)
    return pl.pallas_call(
        first_gather_kernel,
        out_shape=(
            jax.ShapeDtypeStruct((2, 4) + weights.shape[1:], weights.dtype),
            jax.ShapeDtypeStruct((4,) + gains.shape, gains.dtype),
        ),
        in_specs=[hbm] * 2,
        out_specs=(hbm,) * 2,
        scratch_shapes=dma(4, 4, 4, 4, 3, 3, 2),
        compiler_params=pltpu.CompilerParams(collective_id=2, has_side_effects=True),
        cost_estimate=pl.CostEstimate(flops=0, bytes_accessed=60_000_000, transcendentals=0),
    )(weights, gains)


def second_gather(kv, weight, down):
    hbm = pl.BlockSpec(memory_space=pl.ANY)
    return pl.pallas_call(
        second_gather_kernel,
        out_shape=(
            jax.ShapeDtypeStruct((4, 4, 2) + kv.shape, kv.dtype),
            jax.ShapeDtypeStruct((2, 4) + weight.shape[1:], weight.dtype),
            jax.ShapeDtypeStruct((4,) + down.shape, down.dtype),
        ),
        in_specs=[hbm] * 3,
        out_specs=(hbm,) * 3,
        scratch_shapes=dma((5, 4), (5, 4), 4, 4, 4, 4, 16, 16, 3, 3, 3),
        compiler_params=pltpu.CompilerParams(collective_id=3, has_side_effects=True),
        cost_estimate=pl.CostEstimate(flops=0, bytes_accessed=100_000_000, transcendentals=0),
    )(kv, weight, down)


class RingSum:
    def __init__(self, ring, value, parts, far, passed, far_in, near_in, send, recv):
        self.place, self.right, self.left = ring
        self.value, self.parts = value, parts
        self.far, self.passed, self.far_in, self.near_in = far, passed, far_in, near_in
        self.send, self.recv = send, recv
        self.begun = []

    def _go(self, source, target, index, device):
        copy = remote(source, target, self.send.at[index], self.recv.at[index], device)
        copy.start()
        self.begun.append(copy)
        return copy

    def send_far(self):
        top, low = self.parts
        other = lax.rem(self.place + 2, 4)
        for part in self.parts:
            self.far[part] = self.value(other, part).astype(jnp.bfloat16)
        self.far_right = self._go(self.far.at[top], self.far_in.at[top], 0, self.right)
        self.far_left = self._go(self.far.at[low], self.far_in.at[low], 1, self.left)

    def send_right(self):
        top, low = self.parts
        other = lax.rem(self.place + 1, 4)
        self.passed[0, low] = self.value(other, low).astype(jnp.bfloat16)
        self.far_right.wait_recv()
        total = self.value(other, top) + self.far_in[top].astype(jnp.float32)
        self.passed[0, top] = total.astype(jnp.bfloat16)
        self.near_right = self._go(self.passed.at[0], self.near_in.at[0], 2, self.right)

    def send_left(self):
        top, low = self.parts
        other = lax.rem(self.place + 3, 4)
        self.passed[1, top] = self.value(other, top).astype(jnp.bfloat16)
        self.far_left.wait_recv()
        total = self.value(other, low) + self.far_in[low].astype(jnp.float32)
        self.passed[1, low] = total.astype(jnp.bfloat16)
        self.near_left = self._go(self.passed.at[1], self.near_in.at[1], 3, self.left)

    def arrive(self):
        self.near_right.wait_recv()
        self.near_left.wait_recv()

    def total(self, part):
        return (
            self.value(self.place, part)
            + self.near_in[0, part].astype(jnp.float32)
            + self.near_in[1, part].astype(jnp.float32)
        )

    def drain(self):
        for copy in self.begun:
            copy.wait_send()


def ring_scratch(shape):
    return [
        pltpu.VMEM(shape, jnp.bfloat16),
        pltpu.VMEM((2,) + shape, jnp.bfloat16),
        pltpu.VMEM(shape, jnp.bfloat16),
        pltpu.VMEM((2,) + shape, jnp.bfloat16),
        pltpu.SemaphoreType.DMA((4,)),
        pltpu.SemaphoreType.DMA((4,)),
    ]


HALVES = (pl.ds(0, 2), pl.ds(2, 2))


class PlaneSum:
    def __init__(self, rings, parts, theirs, one, two, sib_send, sib_recv):
        self.first, self.second = rings
        self.parts, self.theirs = parts, theirs
        self.c = lax.axis_index("c")
        self.sib_send, self.sib_recv = sib_send, sib_recv
        middle, one, two = one[0], one[1:], two
        self.middle = middle
        shape = middle.shape[1:]
        self.rows = (pl.ds(0, shape[0] // 2), pl.ds(shape[0] // 2, shape[0] // 2))
        self.ring_one = RingSum(self.first, self._both, HALVES, *one)
        self.ring_two = RingSum(self.second, self._middle, self.rows, *two)

    def _both(self, a, part):
        mine = self.parts[self.c, a, part].astype(jnp.float32)
        return mine + self.theirs[a, part].astype(jnp.float32)

    def _middle(self, b, part):
        return self.middle[b, part].astype(jnp.float32)

    def hand(self, k):
        a = lax.rem(self.second[0] + (2, 1, 3, 0)[k], 4)
        copy = remote(
            self.parts.at[1 - self.c, a],
            self.theirs.at[a],
            self.sib_send.at[k],
            self.sib_recv.at[k],
            {"c": 1 - self.c},
        )
        copy.start()
        return copy

    def along_first(self, handed):
        one = self.ring_one
        handed[0].wait_recv()
        one.send_far()
        handed[1].wait_recv()
        one.send_right()
        handed[2].wait_recv()
        one.send_left()
        handed[3].wait_recv()

    def along_second(self):
        one, two = self.ring_one, self.ring_two
        one.arrive()
        for part in HALVES:
            self.middle[part] = one.total(part).astype(jnp.bfloat16)
        two.send_far()
        two.send_right()
        two.send_left()

    def drain(self, handed):
        for copy in handed:
            copy.wait_send()
        self.ring_one.drain()
        self.ring_two.drain()


ORDER = (2, 1, 3, 0)


def fill(plane, left_ref, right_ref):
    c = lax.axis_index("c")
    wide = left_ref.shape[3]

    def product(core, a):
        lhs = left_ref[core, a].reshape(4 * wide, left_ref.shape[4])
        for z in range(4):
            block = multiply(lhs, right_ref[z]).astype(jnp.bfloat16)
            plane.parts[core, a, :, z] = block.reshape(4, wide, block.shape[1])

    handed = []
    for k in range(4):
        product(1 - c, lax.rem(plane.second[0] + ORDER[k], 4))
        handed.append(plane.hand(k))
    for k in range(4):
        product(c, lax.rem(plane.first[0] + ORDER[k], 4))
    return handed


def pairs_sum_kernel(
    parts, ffn, left_ref, right_ref, kv_out, ffn_out, out_ref,
    theirs, middle, products, their_products, products_middle, last, *scratch,
):
    sems, rest = scratch[:4], scratch[4:]
    one, two, three, four, five, six = (rest[6 * k : 6 * k + 6] for k in range(6))
    first, second = plane_rings()
    z_ring = ring_of("z")
    greet((first[1], first[2], second[1], second[2], z_ring[1], z_ring[2], {"c": 1 - lax.axis_index("c")}))
    pairs = PlaneSum((first, second), parts, theirs, (middle,) + one, two, *sems[:2])
    weights = PlaneSum(
        (first, second), products, their_products, (products_middle,) + four, five, *sems[2:]
    )
    handed = [pairs.hand(k) for k in range(4)]
    along_z = RingSum(
        z_ring, lambda i, part: ffn[i, part].astype(jnp.float32), HALVES, *three
    )
    along_z.send_far()
    handed_weights = fill(weights, left_ref, right_ref)
    pairs.along_first(handed)
    weights.along_first(handed_weights)
    along_z.send_right()
    along_z.send_left()
    pairs.along_second()
    weights.along_second()
    pairs.ring_two.arrive()
    for part in pairs.rows:
        kv_out[part] = pairs.ring_two.total(part)
    weights.ring_two.arrive()
    for part in weights.rows:
        last[part] = weights.ring_two.total(part)
    weights_z = RingSum(z_ring, lambda i, part: last[i, part], cut(left_ref.shape[3]), *six)
    weights_z.send_far()
    along_z.arrive()
    for part in HALVES:
        ffn_out[part] = along_z.total(part).astype(jnp.bfloat16)
    weights_z.send_right()
    weights_z.send_left()
    weights_z.arrive()
    for part in weights_z.parts:
        out_ref[part] = weights_z.total(part)
    pairs.drain(handed)
    weights.drain(handed_weights)
    along_z.drain()
    weights_z.drain()


def pairs_sum(parts, ffn, left, right):
    vmem = pl.BlockSpec(memory_space=pltpu.VMEM)
    block, share = parts.shape[3:], ffn.shape[2:]
    weight = (left.shape[3], right.shape[2])
    return pl.pallas_call(
        pairs_sum_kernel,
        out_shape=(
            jax.ShapeDtypeStruct(block, jnp.float32),
            jax.ShapeDtypeStruct((4,) + share, jnp.bfloat16),
            jax.ShapeDtypeStruct(weight, jnp.float32),
        ),
        in_specs=[vmem] * 4,
        out_specs=(vmem,) * 3,
        scratch_shapes=[
            pltpu.VMEM((4, 4) + block, jnp.bfloat16),
            pltpu.VMEM((4,) + block, jnp.bfloat16),
            pltpu.VMEM((2, 4, 4, 4) + weight, jnp.bfloat16),
            pltpu.VMEM((4, 4, 4) + weight, jnp.bfloat16),
            pltpu.VMEM((4, 4) + weight, jnp.bfloat16),
            pltpu.VMEM((4,) + weight, jnp.float32),
        ]
        + dma(4, 4, 4, 4)
        + ring_scratch((4,) + block)
        + ring_scratch(block)
        + ring_scratch((4,) + share)
        + ring_scratch((4, 4) + weight)
        + ring_scratch((4,) + weight)
        + ring_scratch(weight),
        compiler_params=pltpu.CompilerParams(
            collective_id=4, has_side_effects=True, vmem_limit_bytes=60 * 2**20
        ),
    )(parts, ffn, left, right)


def weights_sum_kernel(
    left_ref, right_ref, gain_ref, ffn_ref, out_ref, gain_out, ffn_out, down_out,
    parts, theirs, middle, last, gain_in, gain_now, down_own, *scratch,
):
    sems, rest = scratch[:2], scratch[2:]
    one, two, three, four = (rest[6 * k : 6 * k + 6] for k in range(4))
    gain_send, gain_recv, down_send, down_recv, down_sib_send, down_sib_recv, local = rest[24:]
    x, c = lax.axis_index("x"), lax.axis_index("c")
    first, second = plane_rings()
    z_ring, x_ring, y_ring = ring_of("z"), ring_of("x"), ring_of("y")
    far = {"x": {"x": lax.rem(x + 2, 4)}}
    far["y"] = {"y": lax.rem(lax.axis_index("y") + 2, 4)}
    far["z"] = {"z": lax.rem(lax.axis_index("z") + 2, 4)}
    greet(
        (first[1], first[2], second[1], second[2], z_ring[1], z_ring[2], {"c": 1 - c})
        + (far["x"], far["y"], far["z"])
    )
    along_y = RingSum(
        y_ring,
        lambda i, part: ffn_ref[i, part].astype(jnp.float32),
        cut(ffn_ref.shape[1]),
        *four,
    )
    along_y.send_far()
    third = down_own.shape[0]
    downs = RingGather(
        x_ring, down_own, lambda i: down_out.at[i, c], cut(third), down_send, down_recv
    )
    passing = Passing(down_sib_send, down_sib_recv)
    own = pltpu.make_async_copy(down_own, down_out.at[x, c], local)

    plane = PlaneSum((first, second), parts, theirs, (middle,) + one, two, *sems)
    handed = fill(plane, left_ref, right_ref)
    along_y.send_right()
    along_y.send_left()

    sent = []

    def share(index, devices):
        copies = [
            remote(
                gain_now.at[index],
                gain_in.at[index, k],
                gain_send.at[index, k],
                gain_recv.at[index, k],
                device,
            )
            for k, device in enumerate(devices)
        ]
        for copy in copies:
            copy.start()
        return copies

    def collect(index, copies):
        total = gain_now[index]
        for k, copy in enumerate(copies):
            copy.wait_recv()
            total = total + gain_in[index, k]
        sent.extend(copies)
        return total

    gain_now[0] = gain_ref[...]
    step = share(0, ({"c": 1 - c},))

    gain_now[1] = collect(0, step)
    step = share(1, (x_ring[1], x_ring[2], far["x"]))

    plane.along_first(handed)
    along_y.arrive()
    for part in along_y.parts:
        ffn_out[part] = along_y.total(part).astype(jnp.bfloat16)
    down_own[...] = ffn_out[2 * third : 3 * third]
    downs.near()
    passing.go(down_own, down_out.at[x, c])
    own.start()
    plane.along_second()
    plane.ring_two.arrive()
    for turn in ("from_left", "from_right", "from_far"):
        block = getattr(downs, turn)()
        passing.go(block, block)
    gain_now[2] = collect(1, step)
    step = share(2, (y_ring[1], y_ring[2], far["y"]))
    for part in plane.rows:
        last[part] = plane.ring_two.total(part)
    along_z = RingSum(z_ring, lambda i, part: last[i, part], cut(left_ref.shape[3]), *three)
    along_z.send_far()
    along_z.send_right()
    along_z.send_left()
    gain_now[3] = collect(2, step)
    step = share(3, (z_ring[1], z_ring[2], far["z"]))
    along_z.arrive()
    for part in along_z.parts:
        out_ref[part] = along_z.total(part)
    gain_out[...] = collect(3, step)
    passing.wait()
    own.wait()
    plane.drain(handed)
    along_z.drain()
    along_y.drain()
    downs.drain()
    passing.drain()
    for copy in sent:
        copy.wait_send()


def weights_sum(left, right, gains, ffn):
    vmem = pl.BlockSpec(memory_space=pltpu.VMEM)
    hbm = pl.BlockSpec(memory_space=pl.ANY)
    block = (left.shape[3], right.shape[2])
    share = ffn.shape[1:]
    down = (share[0] // 3, share[1])
    return pl.pallas_call(
        weights_sum_kernel,
        out_shape=(
            jax.ShapeDtypeStruct(block, jnp.float32),
            jax.ShapeDtypeStruct(gains.shape, jnp.float32),
            jax.ShapeDtypeStruct(share, jnp.bfloat16),
            jax.ShapeDtypeStruct((4, 2) + down, jnp.bfloat16),
        ),
        in_specs=[vmem] * 4,
        out_specs=(vmem, vmem, vmem, hbm),
        scratch_shapes=[
            pltpu.VMEM((2, 4, 4, 4) + block, jnp.bfloat16),
            pltpu.VMEM((4, 4, 4) + block, jnp.bfloat16),
            pltpu.VMEM((4, 4) + block, jnp.bfloat16),
            pltpu.VMEM((4,) + block, jnp.float32),
            pltpu.VMEM((4, 3) + gains.shape, jnp.float32),
            pltpu.VMEM((4,) + gains.shape, jnp.float32),
            pltpu.VMEM(down, jnp.bfloat16),
        ]
        + dma(4, 4)
        + ring_scratch((4, 4) + block)
        + ring_scratch((4,) + block)
        + ring_scratch(block)
        + ring_scratch(share)
        + dma((4, 3), (4, 3), 4, 4, 4, 4)
        + [pltpu.SemaphoreType.DMA],
        compiler_params=pltpu.CompilerParams(
            collective_id=5, has_side_effects=True, vmem_limit_bytes=60 * 2**20
        ),
    )(left, right, gains, ffn)


def shards(
    tokens, cotangent, slot_blocks, norm_gains,
    w_query, w_key, w_value, w_output, w_gate, w_up, w_down,
):
    inputs = tokens[0].astype(jnp.float32)
    row_count = inputs.shape[0]
    ctx_index = lax.axis_index(CTX)
    member = lax.axis_index(TEAM)
    mine = lax.dynamic_slice_in_dim(slot_blocks, 2 * ctx_index, 2)
    offsets = jnp.arange(BLK, dtype=jnp.int32)
    local_pos = (mine[:, None] * BLK + offsets[None, :]).reshape(row_count)
    cosine, sine = rope_tables(local_pos)

    kv_parts = [
        w[:, h * HEAD_DIM : (h + 1) * HEAD_DIM] for h in range(KV_HEADS) for w in (w_key, w_value)
    ]
    w_kv = jnp.concatenate(kv_parts, axis=1)
    wide = w_kv.shape[1] // 2
    gain_rows = jnp.pad(norm_gains, (0, 32 * 128 - norm_gains.shape[0])).reshape(32, 128)
    full_kv, gains = first_gather(jnp.stack([w_kv[:, :wide], w_kv[:, wide:]]), gain_rows)
    full_kv = full_kv.reshape(2, D, wide)
    gains = gains.reshape(4, -1)[:, : D // 2].reshape(2 * D).astype(jnp.float32)

    source = jnp.arange(FF // 8, dtype=jnp.int32)
    source = source // (FF // 32) * (FF // 4) + member * (FF // 32) + source % (FF // 32)
    picked = (jnp.arange(FF, dtype=jnp.int32)[:, None] == source[None, :]).astype(jnp.bfloat16)
    my_gate_up = jnp.stack(
        [multiply(w_gate, picked).astype(jnp.bfloat16), multiply(w_up, picked).astype(jnp.bfloat16)]
    )
    my_down = lax.dynamic_slice_in_dim(w_down, member * (FF // 32), FF // 32)
    upstream_low = cotangent[0]
    gate_up = lax.all_gather(my_gate_up, "z", axis=1, tiled=True)
    full_output = lax.all_gather(w_output, "z", axis=0, tiled=True)
    team_upstream = lax.all_gather(cotangent, TEAM, axis=0, tiled=True)
    my_query = jnp.stack([w_query[:, : D // 2], w_query[:, D // 2 :]])
    gain_first, gain_second = gains[:D], gains[D:]

    root_first = lax.rsqrt(jnp.mean(inputs * inputs, axis=-1, keepdims=True) + epsilon)
    normed_first = (inputs * root_first * gain_first).astype(jnp.bfloat16)
    raw_kv = jnp.concatenate(
        [multiply(normed_first, full_kv[0]), multiply(normed_first, full_kv[1])], axis=1
    )
    pairs = raw_kv.reshape(row_count, KV_HEADS, 2, HEAD_DIM)
    keys = rotate(pairs[:, :, 0], cosine, sine)
    packed = jnp.stack([keys, pairs[:, :, 1]], axis=2).astype(jnp.bfloat16)
    packed = packed.reshape(row_count, KV_HEADS * PAIR)
    gathered, full_query, down = second_gather(packed, my_query, my_down)
    down = down.reshape(FF // 8, D)
    gathered = gathered.reshape(64, BLK, KV_HEADS * PAIR)
    full_query = full_query.reshape(2, D, D // 2)
    raw = jnp.concatenate(
        [multiply(normed_first, full_query[0]), multiply(normed_first, full_query[1])], axis=1
    )
    queries = rotate(raw.reshape(row_count, HEADS, HEAD_DIM), cosine, sine)
    query_rows = by_group(queries.astype(jnp.bfloat16) * jnp.bfloat16(0.125), 0)
    out_turned, lse = attend_forward(slot_blocks, mine, query_rows, gathered)
    attended = from_group(out_turned).reshape(row_count, D).astype(jnp.bfloat16)
    middle = inputs + multiply(attended, full_output)

    root_second = lax.rsqrt(jnp.mean(middle * middle, axis=-1, keepdims=True) + epsilon)
    normed_second = (middle * root_second * gain_second).astype(jnp.bfloat16)
    grad_normed_second, partial, grad_ffn = feed_forward(
        normed_second, team_upstream.reshape(4, 2, row_count, D), gate_up, down
    )
    down_sum = lax.psum_scatter(
        partial.reshape(8, row_count, D), TEAM, scatter_dimension=0, tiled=True
    )

    norm_part, gain_grad_second = norm_backward(
        grad_normed_second, middle, root_second, gain_second
    )
    grad_middle = upstream_low.astype(jnp.float32) + norm_part
    middle_low = grad_middle.astype(jnp.bfloat16)

    grad_attended = multiply_transposed(middle_low, full_output).astype(jnp.bfloat16)

    grad_rows = by_group(grad_attended.reshape(row_count, HEADS, HEAD_DIM), HEAD_DIM)
    query_turned, grad_pairs = attend_backward(
        slot_blocks, mine, query_rows, grad_rows, out_turned, lse, gathered
    )
    grad_query_raw = rotate(from_group(query_turned), cosine, -sine)
    grad_query_raw = grad_query_raw.reshape(row_count, D).astype(jnp.bfloat16)

    def by_owner(columns):
        columns = columns.reshape((4, 4, 2) + columns.shape[1:])
        return jnp.stack([columns[:, :, 0].swapaxes(0, 1), columns[:, :, 1]])

    above = jnp.pad(grad_query_raw.reshape(row_count, 32, 30), ((0, 0), (0, 0), (0, 34)))
    below = jnp.pad(middle_low.reshape(row_count, 32, 30), ((0, 0), (0, 0), (30, 4)))
    columns = by_owner(jnp.concatenate([above, below], axis=0).transpose(1, 2, 0))
    rows = jnp.concatenate([normed_first, attended], axis=0)
    rows = rows.reshape(2 * row_count, 4, D // 4).swapaxes(0, 1)
    own_pairs, part_ffn, sum_query_output = pairs_sum(grad_pairs, grad_ffn, columns, rows)
    own_pairs = own_pairs.reshape(row_count, KV_HEADS, 2, HEAD_DIM)
    grad_key_raw = rotate(own_pairs[:, :, 0], cosine, -sine)
    grad_kv = jnp.stack([grad_key_raw, own_pairs[:, :, 1]], axis=2)
    grad_kv = grad_kv.reshape(row_count, -1).astype(jnp.bfloat16)
    grad_normed_first = multiply_transposed(grad_query_raw[:, : D // 2], full_query[0])
    grad_normed_first += multiply_transposed(grad_query_raw[:, D // 2 :], full_query[1])
    grad_normed_first += multiply_transposed(grad_kv[:, :wide], full_kv[0])
    grad_normed_first += multiply_transposed(grad_kv[:, wide:], full_kv[1])
    norm_first_part, gain_grad_first = norm_backward(
        grad_normed_first, inputs, root_first, gain_first
    )
    input_grad = grad_middle + norm_first_part

    kv_columns = grad_kv.reshape(row_count, KV_HEADS, 2, HEAD_DIM)
    k_columns = kv_columns[:, :, 0].reshape(row_count, 32, 10)
    v_columns = kv_columns[:, :, 1].reshape(row_count, 32, 10)
    columns = jnp.concatenate([k_columns, v_columns], axis=2)
    columns = jnp.pad(columns, ((0, 0), (0, 0), (0, 12))).transpose(1, 2, 0)
    gain_grads = jnp.pad(
        jnp.concatenate([gain_grad_first, gain_grad_second]), (0, 128)
    ).reshape(16, 128)
    sum_pair, sum_gains, sum_ffn, team_down = weights_sum(
        by_owner(columns), rows[:, :row_count], gain_grads, part_ffn
    )
    down_sum, sum_pair = lax.optimization_barrier((down_sum, sum_pair))
    layer_out = (middle + down_sum[0].astype(jnp.float32)).astype(jnp.bfloat16)[None]
    sum_query_output, sum_pair = sum_query_output.T, sum_pair.T
    ffn_columns = sum_ffn[:160].T.astype(jnp.float32)
    sum_down = lax.dynamic_slice_in_dim(
        team_down.reshape(FF // 4, D // 4), member * 30, 30, axis=1
    ).astype(jnp.float32)
    place = (ctx_index * 4 + lax.axis_index("z")) * 15
    return (
        layer_out,
        input_grad[None],
        lax.dynamic_slice_in_dim(sum_gains.reshape(-1), place, 15),
        sum_query_output[:, :30],
        sum_pair[:, :10],
        sum_pair[:, 10:20],
        sum_query_output[:, 30:60],
        ffn_columns[:, :80],
        ffn_columns[:, 80:],
        sum_down,
    )


def solution(mesh):
    fine = Mesh(mesh.devices.reshape(4, 4, 2, 4), ALL)
    weight = P("z", None)
    return jax.shard_map(
        shards,
        mesh=fine,
        in_specs=(
            P("z", CTX, None),
            P("z", CTX, None),
            P(),
            P("z"),
        )
        + (weight,) * 7,
        out_specs=(
            P("z", CTX, None),
            P("z", CTX, None),
            P(ALL),
        )
        + (P("z", CTX),) * 7,
        check_vma=False,
    )
```

time: 918 us -> 313 us (0.34)
  waiting for transfers between devices: 399 us -> 1.42 us
  Pallas kernels: 0 us -> 237 us
  blocking collectives: 219 us -> 0 us
  matrix products: 143 us -> 9.92 us
  local copies, waits for them, and re-layouts: 79.3 us -> 35.2 us
  other arithmetic: 43.1 us -> 11.9 us
  starting transfers between devices: 9.68 us -> 0.16 us
    pallas_call x0 -> x7, Pallas kernels: none -> 237 us  [the longest x1 53.4 us: pairs_sum(): pl.pallas_call(pairs_sum_kernel, out_shape=(jax.ShapeDtypeStruct(block, j...]
    unnamed x32 -> x4, waiting for transfers between devices: 205 us -> 1.41 us
    all_gather x6 -> x3, waiting for transfers between devices: 194 us -> 0.01 us  [the longest x1 0.01 us: shards(): full_output = lax.all_gather(w_output, 'z', axis=0, tiled=True)]
    unnamed x4 -> x0, blocking collectives: 187 us -> none
    dot_general x34 -> x5, matrix products: 102 us -> 4.03 us  [multiply_transposed(): return lax.dot_general(left, right, NT, preferred_element_type=jnp.float32)]
    unnamed x219 -> x71, local copies, waits for them, and re-layouts: 67.5 us -> 7.59 us
    dot_general x17 -> x7, matrix products: 40.5 us -> 5.89 us  [multiply(): return jnp.dot(left, right, preferred_element_type=jnp.float32)]
    all_gather x2 -> x0, blocking collectives: 32.8 us -> none  [the longest x1 17.7 us: shards(): lax.all_gather(w_value, 'fsdp', axis=0, tiled=True)]
  transfers between devices with their start and end apart: 23 -> 4, of which waited for: 11 -> 0; matrix products, arithmetic and copies ran while one was open for 36% -> 17% of each run, Pallas kernels for 0% -> 65%
where the time goes in v1:
time: 313 us; the launch traced here: 310 us
  Pallas kernels  237 us (76%)
  local copies, waits for them, and re-layouts  35.2 us (11%)
  between operations  14.9 us (5%)
  other arithmetic  11.9 us (4%)
  matrix products  9.92 us (3%)
    pallas_call x1, Pallas kernels, pairs_sum(): pl.pallas_call(pairs_sum_kernel, out_shape=(jax.ShapeDtypeStruct(block, j...  53.4 us
    pallas_call x1, Pallas kernels, weights_sum(): pl.pallas_call(weights_sum_kernel, out_shape=(jax.ShapeDtypeStruct(block,...  40.5 us
    pallas_call x1, Pallas kernels, feed_forward(): pl.pallas_call(ffn_kernel, out_shape=(jax.ShapeDtypeStruct((2 * BLK, D),...  35.9 us
    pallas_call x1, Pallas kernels, second_gather(): pl.pallas_call(second_gather_kernel, out_shape=(jax.ShapeDtypeStruct((4,...  32.7 us
    pallas_call x1, Pallas kernels, attend_forward(): pl.pallas_call(forward_kernel, out_shape=(jax.ShapeDtypeStruct((2, KV_HEA...  28.7 us
    pallas_call x1, Pallas kernels, attend_backward(): pl.pallas_call(backward_kernel, out_shape=(jax.ShapeDtypeStruct((2, KV_HE...  26.4 us
    pallas_call x1, Pallas kernels, first_gather(): pl.pallas_call(first_gather_kernel, out_shape=(jax.ShapeDtypeStruct((2, 4...  19.1 us
    unnamed x71, local copies, waits for them, and re-layouts  7.59 us
  transfers between devices with their start and end apart: 4, of which 0 were waited for; matrix products, arithmetic and copies ran while one was open for 17% of the time, Pallas kernels for 65%

profile of v1, /device:TPU:0, one launch (start us, length us, event | category | flops | bytes accessed | tf_op | source)
XLA Modules:
  0.0 310.2 jit_solution(17749992693677715434)
XLA Ops:
  14.9 19.1 %shard_map.186 = (bf16[2,4,240,320]{3,2,1,0:T(8,128)(2,1)}, bf16[4,32,128]{2,1,0:T(8,128)(2,1)}) custom-call(bf16[2,240,320]{2,1,0:T(8,128)(2,1)} %pad_maximum_fusion.3.w_ref, bf16[32,128]{1,0:T(8,128)(2,1)} %pad_bitcast_fusion.gain_ref), custom_call_target="tpu_custom_call" | custom-call | bytes 60000000 | tf_op jit(solution)/shard_map/pallas_call | solution.py:661
  34.1 1.5 fusion.64
  39.4 1.2 constant_dynamic-slice_fusion.1
  42.2 32.7 %shard_map.187 = (bf16[4,4,2,128,640]{4,3,2,1,0:T(8,128)(2,1)}, bf16[2,4,240,480]{3,2,1,0:T(8,128)(2,1)}, bf16[4,80,960]{2,1,0:T(8,128)(2,1)}) custom-call(bf16[128,640]{1,0:T(8,128)(2,1)} %copy.155.kv_ref, bf16[2,240,480]{2,1,0:T(8,128)(2,1)} %pad_maximum_fusion.1.o_ref, bf16[80,960]{1,0:T(8,128)(2,1)} %copy.200.down_ref), custom_call_target="tpu_custom_call" | custom-call | bytes 100000000 | tf_op jit(solution)/shard_map/pallas_call | solution.py:677
  75.0 1.7 fusion.63
  80.3 28.7 %shard_map.188 = (f32[2,5,64,256]{3,2,1,0:T(8,128)S(1)}, f32[2,5,1,256]{3,2,1,0:T(1,128)S(1)}) custom-call(s32[64]{0:T(128)S(1)} %copy-done.2, s32[2]{0:T(128)S(1)} %get-tuple-element.99.mine_ref, bf16[2,5,256,128]{3,2,1,0:T(8,128)(2,1)S(1)} %pad.29.q_ref, bf16[64,64,640]{2,1,0:T(8,128)(2,1)} %bitcast.213), custom_call_target="tpu_custom_call" | custom-call | flops 10000000000 | bytes 8000000 | tf_op jit(solution)/shard_map/pallas_call | solution.py:201
  109.3 1.0 copy.158
  113.2 2.2 multiply_reduce_fusion.2
  116.2 3.9 %copy.160 = bf16[8,128,960]{2,1,0:T(8,128)(2,1)} copy(bf16[8,128,960]{1,2,0:T(8,128)(2,1)} %all-gather.6.cloned.1.call-done) | data formatting | bytes 3932160 | tf_op jit(solution)/shard_map/all_gather | solution.py:1099
  120.1 35.9 %shard_map.189 = (f32[128,960]{1,0:T(8,128)}, bf16[4,2,128,960]{3,2,1,0:T(8,128)(2,1)}, bf16[4,4,240,240]{3,2,1,0:T(8,128)(2,1)}) custom-call(bf16[128,960]{1,0:T(8,128)(2,1)} %multiply_convert_fusion.1.h_ref, bf16[4,2,128,960]{3,2,1,0:T(8,128)(2,1)} %bitcast.187, bf16[2,960,320]{2,1,0:T(8,128)(2,1)} %all-gather.8.cloned.1.call-done.gate_up_ref, ...), custom_call_target="tpu_custom_call" | custom-call | flops 6000000000 | bytes 12000000 | tf_op jit(solution)/shard_map/pallas_call | solution.py:421
  156.1 1.0 copy-done.12
  157.3 1.0 fusion.62
  159.1 2.2 convolution_convert_fusion
  161.6 1.0 copy.164
  162.8 1.7 reshape.354
  164.5 26.4 %shard_map.190 = (f32[2,5,64,256]{3,2,1,0:T(8,128)S(1)}, bf16[2,4,4,128,640]{4,3,2,1,0:T(8,128)(2,1)}) custom-call(s32[64]{0:T(128)S(1)} %copy-done.2, s32[2]{0:T(128)S(1)} %get-tuple-element.99.mine_ref, bf16[2,5,256,128]{3,2,1,0:T(8,128)(2,1)S(1)} %pad.29.q_ref, bf16[2,5,256,128]{3,2,1,0:T(8,128)(2,1)S(1)} %pad.30.do_ref, ...), custom_call_target="tpu_custom_call" | custom-call | flops 20000000000 | bytes 12000000 | tf_op jit(solution)/shard_map/pallas_call | solution.py:228
  191.3 1.1 copy.166
  193.6 1.1 pad_maximum_fusion.left_ref
  194.7 53.4 %shard_map.191 = (f32[128,640]{1,0:T(8,128)}, bf16[4,240,240]{2,1,0:T(8,128)(2,1)}, f32[64,240]{1,0:T(8,128)}) custom-call(bf16[2,4,4,128,640]{4,3,2,1,0:T(8,128)(2,1)} %get-tuple-element.40.parts, bf16[4,4,240,240]{3,2,1,0:T(8,128)(2,1)} %get-tuple-element.41.ffn, bf16[2,4,4,64,256]{4,3,2,1,0:T(8,128)(2,1)} %pad_maximum_fusion.left_ref, ...), custom_call_target="tpu_custom_call" | custom-call | tf_op jit(solution)/shard_map/pallas_call | solution.py:893
  248.2 1.2 copy.174
  255.1 40.5 %shard_map.192 = (f32[32,240]{1,0:T(8,128)}, f32[16,128]{1,0:T(8,128)}, bf16[240,240]{1,0:T(8,128)(2,1)}, bf16[4,2,80,240]{3,2,1,0:T(8,128)(2,1)}) custom-call(bf16[2,4,4,32,128]{4,3,2,1,0:T(8,128)(2,1)} %pad_maximum_fusion.6.left_ref, bf16[4,128,240]{2,1,0:T(8,128)(2,1)} %slice.261.right_ref, f32[16,128]{1,0:T(8,128)} %fusion.42.gain_ref, ...), custom_call_target="tpu_custom_call" | custom-call | tf_op jit(solution)/shard_map/pallas_call | solution.py:1034
  295.7 1.1 constant_dynamic-slice_fusion
  297.5 1.3 dynamic_slice.14
  301.0 1.0 fusion.33
  (174 shorter events, 33.4 us)
Async XLA Ops:
  7.2 1.6 copy-start
  7.2 106.0 %all-gather.4.cloned.1.call-start = ((), (), s32[]{:S(2)}) async-start(), calls=%async_computation.1 | async-start | bytes 2457600 | tf_op jit(solution)/shard_map/all_gather | solution.py:1098
  7.9 108.3 %all-gather.6.cloned.1.call-start = ((), (), s32[]{:S(2)}) async-start(), calls=%async_computation.2 | async-start | bytes 2211840 | tf_op jit(solution)/shard_map/all_gather | solution.py:1099
  8.7 111.4 %all-gather.8.cloned.1.call-start = ((), (), s32[]{:S(2)}) async-start(), calls=%async_computation.3 | async-start | bytes 1843200 | tf_op jit(solution)/shard_map/all_gather | solution.py:1097
  8.8 1.3 copy-start.25
  10.0 1.9 copy-start.19
  10.9 2.3 copy-start.24
  11.9 289.1 %reduce-scatter.2.cloned.1.call-start = ((), (), s32[]{:S(2)}) async-start(), calls=%async_computation.4 | async-start | bytes 2359296 | tf_op jit(solution)/shard_map/reduce_scatter | solution.py:1130
  14.1 21.5 %copy-start.18 = (bf16[1,128,960]{1,2,0:T(8,128)(2,1)S(1)}, bf16[1,128,960]{1,2,0:T(8,128)(2,1)}, u32[]{:S(2)}) copy-start(bf16[1,128,960]{1,2,0:T(8,128)(2,1)} %param.11) | copy-start | bytes 737284
  34.1 1.7 copy-start.23
  35.6 1.5 copy-start.7
  35.6 1.5 copy-start.9
  35.8 1.3 copy-start.16
  36.1 1.9 copy-start.2
  36.5 2.7 copy-start.17
  76.7 1.3 copy-start.5
  112.4 3.9 %copy-start.11 = (bf16[4,256,240]{2,1,0:T(8,128)(2,1)}, bf16[4,256,240]{2,1,0:T(8,128)(2,1)S(1)}, u32[]{:S(2)}) copy-start(bf16[4,256,240]{2,1,0:T(8,128)(2,1)S(1)} %maximum_bitcast_fusion.right_ref) | copy-start | bytes 1474564
  156.1 1.2 copy-start.14
  248.2 1.6 copy-start.10
  249.6 1.4 copy-start.6
  249.8 1.7 copy-start.4
  252.7 46.1 %copy-start.21 = (f32[64,240]{1,0:T(8,128)S(1)}, f32[64,240]{1,0:T(8,128)}, u32[]{:S(2)}) copy-start(f32[64,240]{1,0:T(8,128)} %get-tuple-element.48) | copy-start | bytes 184324
  255.1 48.4 %copy-start.1 = (bf16[240,2560]{1,0:T(8,128)(2,1)S(1)}, bf16[240,2560]{1,0:T(8,128)(2,1)}, u32[]{:S(2)}) copy-start(bf16[240,2560]{1,0:T(8,128)(2,1)} %param.20) | copy-start | bytes 3686404
  295.6 7.3 %copy-start.22 = (f32[32,240]{1,0:T(8,128)S(1)}, f32[32,240]{1,0:T(8,128)}, u32[]{:S(2)}) copy-start(f32[32,240]{1,0:T(8,128)} %get-tuple-element.49) | copy-start | bytes 92164
  (6 other events, 6.6 us)
Sparse Core Ops, SparseCore 0:
  9.7 34.4 all-gather.3
  45.9 26.6 all-gather.5
  74.2 25.6 all-gather.7
  156.2 31.3 reduce-scatter.1

commit v2 on v1

--- a/solution.py
+++ b/solution.py
@@ -285,9 +285,9 @@
 
 
 def ffn_kernel(
-    h_ref, cot_ref, gate_up_ref, down_ref,
+    h_ref, cot_columns_ref, gate_up_ref, down_ref,
     dh_ref, partial_ref, grads_ref,
-    rows, grad, hid, dgate, dup, mine, from_sibling, kept, halves, passed, arrived,
+    rows, cot_ref, grad, hid, dgate, dup, mine, from_sibling, kept, halves, passed, arrived,
     gather_send, gather_recv, sib_send, sib_recv, ring_send, ring_recv,
 ):
     x, c = lax.axis_index("x"), lax.axis_index("c")
@@ -308,6 +308,13 @@
     for copy in first:
         copy.start()
     from_left, from_right, from_far = rows.at[left, c], rows.at[right, c], rows.at[across, c]
+    place = lax.broadcasted_iota(jnp.int32, (2 * BLK, 2 * BLK), 0)
+    across_place = lax.broadcasted_iota(jnp.int32, (2 * BLK, 2 * BLK), 1)
+    identity = jnp.where(place == across_place, 1.0, 0.0).astype(jnp.bfloat16)
+    for chip in range(4):
+        for core in range(2):
+            turned = multiply_transposed(identity, cot_columns_ref[chip, core])
+            cot_ref[chip, core] = turned.astype(jnp.bfloat16)
     gate_w, up_w = gate_up_ref[0], gate_up_ref[1]
     down_w = down_ref[...]
 
@@ -428,6 +435,7 @@
         in_specs=[vmem] * 4,
         out_specs=(vmem,) * 3,
         scratch_shapes=[
+            pltpu.VMEM((4, 2, 2 * BLK, D), jnp.bfloat16),
             pltpu.VMEM((4, 2, 2 * BLK, D), jnp.bfloat16),
             pltpu.VMEM((width, D), jnp.float32),
             pltpu.VMEM((4, 4 * BLK, width), jnp.bfloat16),
@@ -824,11 +832,14 @@
     c = lax.axis_index("c")
     wide = left_ref.shape[3]
 
+    rows = plane.parts.shape[-1]
+
     def product(core, a):
         lhs = left_ref[core, a].reshape(4 * wide, left_ref.shape[4])
+        block = multiply(lhs, right_ref[...]).astype(jnp.bfloat16)
         for z in range(4):
-            block = multiply(lhs, right_ref[z]).astype(jnp.bfloat16)
-            plane.parts[core, a, :, z] = block.reshape(4, wide, block.shape[1])
+            piece = block[:, z * LANES : z * LANES + rows]
+            plane.parts[core, a, :, z] = piece.reshape(4, wide, rows)
 
     handed = []
     for k in range(4):
@@ -889,7 +900,7 @@
 def pairs_sum(parts, ffn, left, right):
     vmem = pl.BlockSpec(memory_space=pltpu.VMEM)
     block, share = parts.shape[3:], ffn.shape[2:]
-    weight = (left.shape[3], right.shape[2])
+    weight = (left.shape[3], D // 4)
     return pl.pallas_call(
         pairs_sum_kernel,
         out_shape=(
@@ -921,22 +932,22 @@
 
 
 def weights_sum_kernel(
-    left_ref, right_ref, gain_ref, ffn_ref, out_ref, gain_out, ffn_out, down_out,
-    parts, theirs, middle, last, gain_in, gain_now, down_own, *scratch,
+    left_ref, right_ref, ffn_ref, out_ref, ffn_out, down_out,
+    parts, theirs, middle, last, down_own, *scratch,
 ):
     sems, rest = scratch[:2], scratch[2:]
     one, two, three, four = (rest[6 * k : 6 * k + 6] for k in range(4))
-    gain_send, gain_recv, down_send, down_recv, down_sib_send, down_sib_recv, local = rest[24:]
+    down_send, down_recv, local = rest[24:]
     x, c = lax.axis_index("x"), lax.axis_index("c")
     first, second = plane_rings()
-    z_ring, x_ring, y_ring = ring_of("z"), ring_of("x"), ring_of("y")
-    far = {"x": {"x": lax.rem(x + 2, 4)}}
-    far["y"] = {"y": lax.rem(lax.axis_index("y") + 2, 4)}
-    far["z"] = {"z": lax.rem(lax.axis_index("z") + 2, 4)}
-    greet(
-        (first[1], first[2], second[1], second[2], z_ring[1], z_ring[2], {"c": 1 - c})
-        + (far["x"], far["y"], far["z"])
-    )
+    z_ring, y_ring = ring_of("z"), ring_of("y")
+    team = [
+        {"x": lax.rem(x + step, 4), "c": (1 - c) if swap else c}
+        for swap in (0, 1)
+        for step in range(4)
+        if step + swap > 0
+    ]
+    greet([y_ring[1], y_ring[2], z_ring[1], z_ring[2]] + team)
     along_y = RingSum(
         y_ring,
         lambda i, part: ffn_ref[i, part].astype(jnp.float32),
@@ -944,110 +955,65 @@
         *four,
     )
     along_y.send_far()
-    third = down_own.shape[0]
-    downs = RingGather(
-        x_ring, down_own, lambda i: down_out.at[i, c], cut(third), down_send, down_recv
-    )
-    passing = Passing(down_sib_send, down_sib_recv)
-    own = pltpu.make_async_copy(down_own, down_out.at[x, c], local)
-
     plane = PlaneSum((first, second), parts, theirs, (middle,) + one, two, *sems)
     handed = fill(plane, left_ref, right_ref)
     along_y.send_right()
     along_y.send_left()
-
-    sent = []
-
-    def share(index, devices):
-        copies = [
-            remote(
-                gain_now.at[index],
-                gain_in.at[index, k],
-                gain_send.at[index, k],
-                gain_recv.at[index, k],
-                device,
-            )
-            for k, device in enumerate(devices)
-        ]
-        for copy in copies:
-            copy.start()
-        return copies
-
-    def collect(index, copies):
-        total = gain_now[index]
-        for k, copy in enumerate(copies):
-            copy.wait_recv()
-            total = total + gain_in[index, k]
-        sent.extend(copies)
-        return total
-
-    gain_now[0] = gain_ref[...]
-    step = share(0, ({"c": 1 - c},))
-
-    gain_now[1] = collect(0, step)
-    step = share(1, (x_ring[1], x_ring[2], far["x"]))
-
     plane.along_first(handed)
     along_y.arrive()
     for part in along_y.parts:
         ffn_out[part] = along_y.total(part).astype(jnp.bfloat16)
+    third = down_own.shape[0]
     down_own[...] = ffn_out[2 * third : 3 * third]
-    downs.near()
-    passing.go(down_own, down_out.at[x, c])
+    own = pltpu.make_async_copy(down_own, down_out.at[x, c], local)
     own.start()
+    downs = [
+        remote(down_own, down_out.at[x, c], down_send.at[k], down_recv.at[k], device)
+        for k, device in enumerate(team)
+    ]
+    for copy in downs:
+        copy.start()
     plane.along_second()
     plane.ring_two.arrive()
-    for turn in ("from_left", "from_right", "from_far"):
-        block = getattr(downs, turn)()
-        passing.go(block, block)
-    gain_now[2] = collect(1, step)
-    step = share(2, (y_ring[1], y_ring[2], far["y"]))
     for part in plane.rows:
         last[part] = plane.ring_two.total(part)
     along_z = RingSum(z_ring, lambda i, part: last[i, part], cut(left_ref.shape[3]), *three)
     along_z.send_far()
     along_z.send_right()
     along_z.send_left()
-    gain_now[3] = collect(2, step)
-    step = share(3, (z_ring[1], z_ring[2], far["z"]))
     along_z.arrive()
     for part in along_z.parts:
         out_ref[part] = along_z.total(part)
-    gain_out[...] = collect(3, step)
-    passing.wait()
     own.wait()
+    for copy in downs:
+        copy.wait_recv()
     plane.drain(handed)
     along_z.drain()
     along_y.drain()
-    downs.drain()
-    passing.drain()
-    for copy in sent:
+    for copy in downs:
         copy.wait_send()
 
 
-def weights_sum(left, right, gains, ffn):
+def weights_sum(left, right, ffn):
     vmem = pl.BlockSpec(memory_space=pltpu.VMEM)
     hbm = pl.BlockSpec(memory_space=pl.ANY)
-    block = (left.shape[3], right.shape[2])
+    block = (left.shape[3], D // 4)
     share = ffn.shape[1:]
     down = (share[0] // 3, share[1])
     return pl.pallas_call(
         weights_sum_kernel,
         out_shape=(
             jax.ShapeDtypeStruct(block, jnp.float32),
-            jax.ShapeDtypeStruct(gains.shape, jnp.float32),
             jax.ShapeDtypeStruct(share, jnp.bfloat16),
             jax.ShapeDtypeStruct((4, 2) + down, jnp.bfloat16),
         ),
-        in_specs=[vmem] * 4,
-        out_specs=(vmem, vmem, vmem, hbm),
+        in_specs=[vmem] * 3,
+        out_specs=(vmem, vmem, hbm),
         scratch_shapes=[
             pltpu.VMEM((2, 4, 4, 4) + block, jnp.bfloat16),
             pltpu.VMEM((4, 4, 4) + block, jnp.bfloat16),
             pltpu.VMEM((4, 4) + block, jnp.bfloat16),
             pltpu.VMEM((4,) + block, jnp.float32),
-            pltpu.VMEM((4, 3) + gains.shape, jnp.float32),
-            pltpu.VMEM((4,) + gains.shape, jnp.float32),
             pltpu.VMEM(down, jnp.bfloat16),
         ]
         + dma(4, 4)
@@ -1055,12 +1021,12 @@
         + ring_scratch((4,) + block)
         + ring_scratch(block)
         + ring_scratch(share)
-        + dma((4, 3), (4, 3), 4, 4, 4, 4)
+        + dma(7, 7)
         + [pltpu.SemaphoreType.DMA],
         compiler_params=pltpu.CompilerParams(
             collective_id=5, has_side_effects=True, vmem_limit_bytes=60 * 2**20
         ),
-    )(left, right, gains, ffn)
+    )(left, right, ffn)
 
 
 def shards(
@@ -1125,7 +1091,10 @@
     root_second = lax.rsqrt(jnp.mean(middle * middle, axis=-1, keepdims=True) + epsilon)
     normed_second = (middle * root_second * gain_second).astype(jnp.bfloat16)
     grad_normed_second, partial, grad_ffn = feed_forward(
-        normed_second, team_upstream.reshape(4, 2, row_count, D), gate_up, down
+        normed_second,
+        team_upstream.swapaxes(1, 2).reshape(4, 2, D, row_count),
+        gate_up,
+        down,
     )
     down_sum = lax.psum_scatter(
         partial.reshape(8, row_count, D), TEAM, scatter_dimension=0, tiled=True
@@ -1153,8 +1122,13 @@
     above = jnp.pad(grad_query_raw.reshape(row_count, 32, 30), ((0, 0), (0, 0), (0, 34)))
     below = jnp.pad(middle_low.reshape(row_count, 32, 30), ((0, 0), (0, 0), (30, 4)))
     columns = by_owner(jnp.concatenate([above, below], axis=0).transpose(1, 2, 0))
-    rows = jnp.concatenate([normed_first, attended], axis=0)
-    rows = rows.reshape(2 * row_count, 4, D // 4).swapaxes(0, 1)
+
+    def by_rows(values):
+        parts = values.reshape(-1, 4, D // 4)
+        return jnp.pad(parts, ((0, 0), (0, 0), (0, LANES - D // 4))).reshape(-1, 4 * LANES)
+
+    normed_rows = by_rows(normed_first)
+    rows = jnp.concatenate([normed_rows, by_rows(attended)], axis=0)
     own_pairs, part_ffn, sum_query_output = pairs_sum(grad_pairs, grad_ffn, columns, rows)
     own_pairs = own_pairs.reshape(row_count, KV_HEADS, 2, HEAD_DIM)
     grad_key_raw = rotate(own_pairs[:, :, 0], cosine, -sine)
@@ -1174,11 +1148,15 @@
     v_columns = kv_columns[:, :, 1].reshape(row_count, 32, 10)
     columns = jnp.concatenate([k_columns, v_columns], axis=2)
     columns = jnp.pad(columns, ((0, 0), (0, 0), (0, 12))).transpose(1, 2, 0)
-    gain_grads = jnp.pad(
-        jnp.concatenate([gain_grad_first, gain_grad_second]), (0, 128)
-    ).reshape(16, 128)
-    sum_pair, sum_gains, sum_ffn, team_down = weights_sum(
-        by_owner(columns), rows[:, :row_count], gain_grads, part_ffn
+    owners = jnp.arange(32, dtype=jnp.int32)
+    mark = (owners[:, None, None] == owners[None, None, :]) & (owners[None, :, None] == 20)
+    columns = jnp.concatenate([columns, mark.astype(jnp.bfloat16)], axis=2)
+    gain_rows = jnp.concatenate([gain_grad_first, gain_grad_second]).astype(jnp.bfloat16)
+    gain_rows = jnp.pad(gain_rows.reshape(32, 4, 15), ((0, 0), (0, 0), (0, LANES - 15)))
+    sum_pair, sum_ffn, team_down = weights_sum(
+        by_owner(columns),
+        jnp.concatenate([normed_rows, gain_rows.reshape(32, 4 * LANES)], axis=0),
+        part_ffn,
     )
     down_sum, sum_pair = lax.optimization_barrier((down_sum, sum_pair))
     layer_out = (middle + down_sum[0].astype(jnp.float32)).astype(jnp.bfloat16)[None]
@@ -1187,11 +1165,10 @@
     sum_down = lax.dynamic_slice_in_dim(
         team_down.reshape(FF // 4, D // 4), member * 30, 30, axis=1
     ).astype(jnp.float32)
-    place = (ctx_index * 4 + lax.axis_index("z")) * 15
     return (
         layer_out,
         input_grad[None],
-        lax.dynamic_slice_in_dim(sum_gains.reshape(-1), place, 15),
+        sum_pair[:15, 20],
         sum_query_output[:, :30],
         sum_pair[:, :10],
         sum_pair[:, 10:20],

time: 313 us -> 311 us (level)
  Pallas kernels: 237 us -> 231 us
    pallas_call x1, Pallas kernels: 40.5 us -> 35.2 us  [weights_sum(): pl.pallas_call(weights_sum_kernel, out_shape=(jax.ShapeDtypeStruct(block,...]
    all_gather x1 -> x0, local copies, waits for them, and re-layouts: 3.87 us -> none  [shards(): team_upstream = lax.all_gather(cotangent, TEAM, axis=0, tiled=True)]
    unnamed x71 -> x83, local copies, waits for them, and re-layouts: 7.59 us -> 8.11 us
  transfers between devices with their start and end apart: 4 -> 4, of which waited for: 0 -> 0; matrix products, arithmetic and copies ran while one was open for 17% -> 17% of each run, Pallas kernels for 65% -> 64%
where the time goes in v2:
time: 311 us; the launch traced here: 308 us
  Pallas kernels  231 us (74%)
  local copies, waits for them, and re-layouts  34.5 us (11%)
  between operations  14.9 us (5%)
  other arithmetic  14.4 us (5%)
  matrix products  10.8 us (3%)
    pallas_call x1, Pallas kernels, pairs_sum(): pl.pallas_call(pairs_sum_kernel, out_shape=(jax.ShapeDtypeStruct(block, j...  52.9 us
    pallas_call x1, Pallas kernels, feed_forward(): pl.pallas_call(ffn_kernel, out_shape=(jax.ShapeDtypeStruct((2 * BLK, D),...  35.4 us
    pallas_call x1, Pallas kernels, weights_sum(): pl.pallas_call(weights_sum_kernel, out_shape=(jax.ShapeDtypeStruct(block,...  35.2 us
    pallas_call x1, Pallas kernels, second_gather(): pl.pallas_call(second_gather_kernel, out_shape=(jax.ShapeDtypeStruct((4,...  33.6 us
    pallas_call x1, Pallas kernels, attend_forward(): pl.pallas_call(forward_kernel, out_shape=(jax.ShapeDtypeStruct((2, KV_HEA...  27.9 us
    pallas_call x1, Pallas kernels, attend_backward(): pl.pallas_call(backward_kernel, out_shape=(jax.ShapeDtypeStruct((2, KV_HE...  26.4 us
    pallas_call x1, Pallas kernels, first_gather(): pl.pallas_call(first_gather_kernel, out_shape=(jax.ShapeDtypeStruct((2, 4...  20 us
    unnamed x83, local copies, waits for them, and re-layouts  8.11 us
  transfers between devices with their start and end apart: 4, of which 0 were waited for; matrix products, arithmetic and copies ran while one was open for 17% of the time, Pallas kernels for 64%

profile of v2, /device:TPU:0, one launch (start us, length us, event | category | flops | bytes accessed | tf_op | source)
XLA Modules:
  0.0 307.5 jit_solution(16773831107752664832)
XLA Ops:
  15.4 20.0 %shard_map.186 = (bf16[2,4,240,320]{3,2,1,0:T(8,128)(2,1)}, bf16[4,32,128]{2,1,0:T(8,128)(2,1)}) custom-call(bf16[2,240,320]{2,1,0:T(8,128)(2,1)} %pad_maximum_fusion.6.w_ref, bf16[32,128]{1,0:T(8,128)(2,1)} %pad_bitcast_fusion.gain_ref), custom_call_target="tpu_custom_call" | custom-call | bytes 60000000 | tf_op jit(solution)/shard_map/pallas_call | solution.py:669
  35.4 1.5 fusion.64
  40.7 1.2 constant_dynamic-slice_fusion.1
  43.5 33.6 %shard_map.187 = (bf16[4,4,2,128,640]{4,3,2,1,0:T(8,128)(2,1)}, bf16[2,4,240,480]{3,2,1,0:T(8,128)(2,1)}, bf16[4,80,960]{2,1,0:T(8,128)(2,1)}) custom-call(bf16[128,640]{1,0:T(8,128)(2,1)} %copy.156.kv_ref, bf16[2,240,480]{2,1,0:T(8,128)(2,1)} %pad_maximum_fusion.4.o_ref, bf16[80,960]{1,0:T(8,128)(2,1)} %copy.205.down_ref), custom_call_target="tpu_custom_call" | custom-call | bytes 100000000 | tf_op jit(solution)/shard_map/pallas_call | solution.py:685
  77.1 1.7 fusion.63
  82.4 27.9 %shard_map.188 = (f32[2,5,64,256]{3,2,1,0:T(8,128)S(1)}, f32[2,5,1,256]{3,2,1,0:T(1,128)S(1)}) custom-call(s32[64]{0:T(128)S(1)} %copy-done.2, s32[2]{0:T(128)S(1)} %get-tuple-element.97.mine_ref, bf16[2,5,256,128]{3,2,1,0:T(8,128)(2,1)S(1)} %pad.36.q_ref, bf16[64,64,640]{2,1,0:T(8,128)(2,1)} %bitcast.220), custom_call_target="tpu_custom_call" | custom-call | flops 10000000000 | bytes 8000000 | tf_op jit(solution)/shard_map/pallas_call | solution.py:201
  115.4 2.2 multiply_reduce_fusion.2
  118.5 35.4 %shard_map.189 = (f32[128,960]{1,0:T(8,128)}, bf16[4,2,128,960]{3,2,1,0:T(8,128)(2,1)}, bf16[4,4,240,240]{3,2,1,0:T(8,128)(2,1)}) custom-call(bf16[128,960]{1,0:T(8,128)(2,1)} %multiply_convert_fusion.h_ref, bf16[4,2,960,128]{3,2,1,0:T(8,128)(2,1)} %bitcast.222, bf16[2,960,320]{2,1,0:T(8,128)(2,1)} %all-gather.8.cloned.1.call-done.gate_up_ref, ...), custom_call_target="tpu_custom_call" | custom-call | flops 6000000000 | bytes 12000000 | tf_op jit(solution)/shard_map/pallas_call | solution.py:428
  155.1 1.4 fusion.62
  157.4 2.2 convolution_convert_fusion
  159.8 1.4 copy.164
  161.3 1.2 pad.37.do_ref
  162.5 1.7 reshape.380
  164.2 26.4 %shard_map.190 = (f32[2,5,64,256]{3,2,1,0:T(8,128)S(1)}, bf16[2,4,4,128,640]{4,3,2,1,0:T(8,128)(2,1)}) custom-call(s32[64]{0:T(128)S(1)} %copy-done.2, s32[2]{0:T(128)S(1)} %get-tuple-element.97.mine_ref, bf16[2,5,256,128]{3,2,1,0:T(8,128)(2,1)S(1)} %pad.36.q_ref, bf16[2,5,256,128]{3,2,1,0:T(8,128)(2,1)S(1)} %pad.37.do_ref, ...), custom_call_target="tpu_custom_call" | custom-call | flops 20000000000 | bytes 12000000 | tf_op jit(solution)/shard_map/pallas_call | solution.py:228
  191.0 1.1 copy.166
  193.4 1.1 pad_maximum_fusion.left_ref
  194.5 52.9 %shard_map.191 = (f32[128,640]{1,0:T(8,128)}, bf16[4,240,240]{2,1,0:T(8,128)(2,1)}, f32[64,240]{1,0:T(8,128)}) custom-call(bf16[2,4,4,128,640]{4,3,2,1,0:T(8,128)(2,1)} %get-tuple-element.39.parts, bf16[4,4,240,240]{3,2,1,0:T(8,128)(2,1)} %get-tuple-element.40.ffn, bf16[2,4,4,64,256]{4,3,2,1,0:T(8,128)(2,1)} %pad_maximum_fusion.left_ref, ...), custom_call_target="tpu_custom_call" | custom-call | tf_op jit(solution)/shard_map/pallas_call | solution.py:904
  247.4 1.2 copy.174
  251.6 1.4 fusion.37
  257.0 35.2 %shard_map.192 = (f32[32,240]{1,0:T(8,128)}, bf16[240,240]{1,0:T(8,128)(2,1)}, bf16[4,2,80,240]{3,2,1,0:T(8,128)(2,1)}) custom-call(bf16[2,4,4,32,160]{4,3,2,1,0:T(8,128)(2,1)} %pad_maximum_fusion.3.left_ref, bf16[160,1024]{1,0:T(8,128)(2,1)} %pad_maximum_fusion.9.right_ref, bf16[4,240,240]{2,1,0:T(8,128)(2,1)} %get-tuple-element.43.ffn_ref), custom_call_target="tpu_custom_call" | custom-call | tf_op jit(solution)/shard_map/pallas_call | solution.py:1003
  292.2 1.1 constant_dynamic-slice_fusion
  296.3 1.2 slice_bitcast_fusion.6
  297.5 1.4 fusion.72
  298.9 1.0 fusion.33
  (196 shorter events, 37.2 us)
Async XLA Ops:
  7.2 108.2 %all-gather.4.cloned.1.call-start = ((), (), s32[]{:S(2)}) async-start(), calls=%async_computation.1 | async-start | bytes 2457600 | tf_op jit(solution)/shard_map/all_gather | solution.py:1064
  7.9 110.5 %all-gather.8.cloned.1.call-start = ((), (), s32[]{:S(2)}) async-start(), calls=%async_computation.3 | async-start | bytes 1843200 | tf_op jit(solution)/shard_map/all_gather | solution.py:1063
  9.8 2.6 copy-start.25
  10.6 1.9 copy-start.26
  10.6 3.1 copy-start.29
  11.6 106.9 %all-gather.6.cloned.1.call-start = ((), (), s32[]{:S(2)}) async-start(), calls=%async_computation.2 | async-start | bytes 2211840 | tf_op jit(solution)/shard_map/all_gather | solution.py:1065
  12.3 284.0 %reduce-scatter.2.cloned.1.call-start = ((), (), s32[]{:S(2)}) async-start(), calls=%async_computation.4 | async-start | bytes 2359296 | tf_op jit(solution)/shard_map/reduce_scatter | solution.py:1099
  14.6 22.3 %copy-start.24 = (bf16[1,128,960]{1,2,0:T(8,128)(2,1)S(1)}, bf16[1,128,960]{1,2,0:T(8,128)(2,1)}, u32[]{:S(2)}) copy-start(bf16[1,128,960]{1,2,0:T(8,128)(2,1)} %param.11) | copy-start | bytes 737284
  35.3 1.7 copy-start.28
  37.4 1.9 copy-start.2
  37.8 2.7 copy-start.23
  113.7 3.9 %copy-start.11 = (bf16[128,1024]{1,0:T(8,128)(2,1)}, bf16[128,1024]{1,0:T(8,128)(2,1)S(1)}, u32[]{:S(2)}) copy-start(bf16[128,1024]{1,0:T(8,128)(2,1)S(1)} %copy.193) | copy-start | bytes 786436
  192.8 54.6 %copy-start.13 = (bf16[128,15,64]{0,2,1:T(8,128)(2,1)}, bf16[128,15,64]{0,2,1:T(8,128)(2,1)S(1)}, u32[]{:S(2)}) copy-start(bf16[128,15,64]{0,2,1:T(8,128)(2,1)S(1)} %maximum_convert_fusion) | copy-start | bytes 737284
  247.4 1.5 copy-start.18
  248.7 2.1 copy-start.10
  248.9 2.3 copy-start.8
  249.0 2.6 copy-start.6
  250.8 2.2 copy-start.4
  250.8 2.2 copy-start.14
  253.6 1.8 copy-start.12
  253.6 2.6 copy-start.19
  253.6 2.6 copy-start.21
  255.4 38.7 %copy-start.27 = (f32[64,240]{1,0:T(8,128)S(1)}, f32[64,240]{1,0:T(8,128)}, u32[]{:S(2)}) copy-start(f32[64,240]{1,0:T(8,128)} %get-tuple-element.47) | copy-start | bytes 184324
  257.0 43.8 %copy-start.1 = (bf16[240,2560]{1,0:T(8,128)(2,1)S(1)}, bf16[240,2560]{1,0:T(8,128)(2,1)}, u32[]{:S(2)}) copy-start(bf16[240,2560]{1,0:T(8,128)(2,1)} %param.20) | copy-start | bytes 3686404
  (11 other events, 13.7 us)
Sparse Core Ops, SparseCore 0:
  9.7 34.6 all-gather.3
  46.0 30.4 all-gather.7
  78.2 24.9 all-gather.5
  154.0 31.7 reduce-scatter.1

commit v3 on v2

--- a/solution.py
+++ b/solution.py
@@ -850,85 +850,55 @@
     return handed
 
 
-def pairs_sum_kernel(
-    parts, ffn, left_ref, right_ref, kv_out, ffn_out, out_ref,
-    theirs, middle, products, their_products, products_middle, last, *scratch,
-):
-    sems, rest = scratch[:4], scratch[4:]
-    one, two, three, four, five, six = (rest[6 * k : 6 * k + 6] for k in range(6))
+def pairs_sum_kernel(parts, ffn, kv_out, ffn_out, theirs, middle, *scratch):
+    sems, rest = scratch[:2], scratch[2:]
+    one, two, three = (rest[6 * k : 6 * k + 6] for k in range(3))
     first, second = plane_rings()
     z_ring = ring_of("z")
     greet((first[1], first[2], second[1], second[2], z_ring[1], z_ring[2], {"c": 1 - lax.axis_index("c")}))
-    pairs = PlaneSum((first, second), parts, theirs, (middle,) + one, two, *sems[:2])
-    weights = PlaneSum(
-        (first, second), products, their_products, (products_middle,) + four, five, *sems[2:]
-    )
+    pairs = PlaneSum((first, second), parts, theirs, (middle,) + one, two, *sems)
     handed = [pairs.hand(k) for k in range(4)]
     along_z = RingSum(
         z_ring, lambda i, part: ffn[i, part].astype(jnp.float32), HALVES, *three
     )
     along_z.send_far()
-    handed_weights = fill(weights, left_ref, right_ref)
     pairs.along_first(handed)
-    weights.along_first(handed_weights)
     along_z.send_right()
     along_z.send_left()
     pairs.along_second()
-    weights.along_second()
     pairs.ring_two.arrive()
     for part in pairs.rows:
         kv_out[part] = pairs.ring_two.total(part)
-    weights.ring_two.arrive()
-    for part in weights.rows:
-        last[part] = weights.ring_two.total(part)
-    weights_z = RingSum(z_ring, lambda i, part: last[i, part], cut(left_ref.shape[3]), *six)
-    weights_z.send_far()
     along_z.arrive()
     for part in HALVES:
         ffn_out[part] = along_z.total(part).astype(jnp.bfloat16)
-    weights_z.send_right()
-    weights_z.send_left()
-    weights_z.arrive()
-    for part in weights_z.parts:
-        out_ref[part] = weights_z.total(part)
     pairs.drain(handed)
-    weights.drain(handed_weights)
     along_z.drain()
-    weights_z.drain()
-
-
-def pairs_sum(parts, ffn, left, right):
+
+
+def pairs_sum(parts, ffn):
     vmem = pl.BlockSpec(memory_space=pltpu.VMEM)
     block, share = parts.shape[3:], ffn.shape[2:]
-    weight = (left.shape[3], D // 4)
     return pl.pallas_call(
         pairs_sum_kernel,
         out_shape=(
             jax.ShapeDtypeStruct(block, jnp.float32),
             jax.ShapeDtypeStruct((4,) + share, jnp.bfloat16),
-            jax.ShapeDtypeStruct(weight, jnp.float32),
-        ),
-        in_specs=[vmem] * 4,
-        out_specs=(vmem,) * 3,
+        ),
+        in_specs=[vmem] * 2,
+        out_specs=(vmem,) * 2,
         scratch_shapes=[
             pltpu.VMEM((4, 4) + block, jnp.bfloat16),
             pltpu.VMEM((4,) + block, jnp.bfloat16),
-            pltpu.VMEM((2, 4, 4, 4) + weight, jnp.bfloat16),
-            pltpu.VMEM((4, 4, 4) + weight, jnp.bfloat16),
-            pltpu.VMEM((4, 4) + weight, jnp.bfloat16),
-            pltpu.VMEM((4,) + weight, jnp.float32),
         ]
-        + dma(4, 4, 4, 4)
+        + dma(4, 4)
         + ring_scratch((4,) + block)
         + ring_scratch(block)
-        + ring_scratch((4,) + share)
-        + ring_scratch((4, 4) + weight)
-        + ring_scratch((4,) + weight)
-        + ring_scratch(weight),
+        + ring_scratch((4,) + share),
         compiler_params=pltpu.CompilerParams(
-            collective_id=4, has_side_effects=True, vmem_limit_bytes=60 * 2**20
-        ),
-    )(parts, ffn, left, right)
+            collective_id=4, has_side_effects=True, vmem_limit_bytes=56 * 2**20
+        ),
+    )(parts, ffn)
 
 
 def weights_sum_kernel(
@@ -1119,17 +1089,11 @@
         columns = columns.reshape((4, 4, 2) + columns.shape[1:])
         return jnp.stack([columns[:, :, 0].swapaxes(0, 1), columns[:, :, 1]])
 
-    above = jnp.pad(grad_query_raw.reshape(row_count, 32, 30), ((0, 0), (0, 0), (0, 34)))
-    below = jnp.pad(middle_low.reshape(row_count, 32, 30), ((0, 0), (0, 0), (30, 4)))
-    columns = by_owner(jnp.concatenate([above, below], axis=0).transpose(1, 2, 0))
-
     def by_rows(values):
         parts = values.reshape(-1, 4, D // 4)
         return jnp.pad(parts, ((0, 0), (0, 0), (0, LANES - D // 4))).reshape(-1, 4 * LANES)
 
-    normed_rows = by_rows(normed_first)
-    rows = jnp.concatenate([normed_rows, by_rows(attended)], axis=0)
-    own_pairs, part_ffn, sum_query_output = pairs_sum(grad_pairs, grad_ffn, columns, rows)
+    own_pairs, part_ffn = pairs_sum(grad_pairs, grad_ffn)
     own_pairs = own_pairs.reshape(row_count, KV_HEADS, 2, HEAD_DIM)
     grad_key_raw = rotate(own_pairs[:, :, 0], cosine, -sine)
     grad_kv = jnp.stack([grad_key_raw, own_pairs[:, :, 1]], axis=2)
@@ -1146,21 +1110,23 @@
     kv_columns = grad_kv.reshape(row_count, KV_HEADS, 2, HEAD_DIM)
     k_columns = kv_columns[:, :, 0].reshape(row_count, 32, 10)
     v_columns = kv_columns[:, :, 1].reshape(row_count, 32, 10)
-    columns = jnp.concatenate([k_columns, v_columns], axis=2)
-    columns = jnp.pad(columns, ((0, 0), (0, 0), (0, 12))).transpose(1, 2, 0)
+    q_columns = grad_query_raw.reshape(row_count, 32, 30)
+    above = jnp.concatenate([q_columns, k_columns, v_columns], axis=2)
+    above = jnp.pad(above, ((0, 0), (0, 0), (0, 46)))
+    below = jnp.pad(middle_low.reshape(row_count, 32, 30), ((0, 0), (0, 0), (50, 16)))
+    columns = jnp.concatenate([above, below], axis=0).transpose(1, 2, 0)
     owners = jnp.arange(32, dtype=jnp.int32)
-    mark = (owners[:, None, None] == owners[None, None, :]) & (owners[None, :, None] == 20)
+    spots = jnp.arange(96, dtype=jnp.int32)
+    mark = (owners[:, None, None] == owners[None, None, :]) & (spots[None, :, None] == 80)
     columns = jnp.concatenate([columns, mark.astype(jnp.bfloat16)], axis=2)
     gain_rows = jnp.concatenate([gain_grad_first, gain_grad_second]).astype(jnp.bfloat16)
     gain_rows = jnp.pad(gain_rows.reshape(32, 4, 15), ((0, 0), (0, 0), (0, LANES - 15)))
-    sum_pair, sum_ffn, team_down = weights_sum(
-        by_owner(columns),
-        jnp.concatenate([normed_rows, gain_rows.reshape(32, 4 * LANES)], axis=0),
-        part_ffn,
-    )
-    down_sum, sum_pair = lax.optimization_barrier((down_sum, sum_pair))
+    gain_rows = gain_rows.reshape(32, 4 * LANES)
+    rows = jnp.concatenate([by_rows(normed_first), by_rows(attended), gain_rows], axis=0)
+    sums, sum_ffn, team_down = weights_sum(by_owner(columns), rows, part_ffn)
+    down_sum, sums = lax.optimization_barrier((down_sum, sums))
     layer_out = (middle + down_sum[0].astype(jnp.float32)).astype(jnp.bfloat16)[None]
-    sum_query_output, sum_pair = sum_query_output.T, sum_pair.T
+    sums = sums.T
     ffn_columns = sum_ffn[:160].T.astype(jnp.float32)
     sum_down = lax.dynamic_slice_in_dim(
         team_down.reshape(FF // 4, D // 4), member * 30, 30, axis=1
@@ -1168,11 +1134,11 @@
     return (
         layer_out,
         input_grad[None],
-        sum_pair[:15, 20],
-        sum_query_output[:, :30],
-        sum_pair[:, :10],
-        sum_pair[:, 10:20],
-        sum_query_output[:, 30:60],
+        sums[:15, 80],
+        sums[:, :30],
+        sums[:, 30:40],
+        sums[:, 40:50],
+        sums[:, 50:80],
         ffn_columns[:, :80],
         ffn_columns[:, 80:],
         sum_down,

time: 311 us -> 310 us (level)
  Pallas kernels: 231 us -> 223 us
  other arithmetic: 14.4 us -> 18.7 us
    pallas_call x1, Pallas kernels: 52.9 us -> 33.9 us  [pairs_sum(): pl.pallas_call(pairs_sum_kernel, out_shape=(jax.ShapeDtypeStruct(block, j...]
    pallas_call x1, Pallas kernels: 35.2 us -> 45.8 us  [weights_sum(): pl.pallas_call(weights_sum_kernel, out_shape=(jax.ShapeDtypeStruct(block,...]
    unnamed x83 -> x72, local copies, waits for them, and re-layouts: 8.11 us -> 8.69 us
  transfers between devices with their start and end apart: 4 -> 4, of which waited for: 0 -> 0; matrix products, arithmetic and copies ran while one was open for 17% -> 16% of each run, Pallas kernels for 64% -> 42%
where the time goes in v3:
time: 310 us; the launch traced here: 305 us
  Pallas kernels  223 us (72%)
  local copies, waits for them, and re-layouts  36.4 us (12%)
  other arithmetic  18.7 us (6%)
  between operations  14.9 us (5%)
  matrix products  11.4 us (4%)
    pallas_call x1, Pallas kernels, weights_sum(): pl.pallas_call(weights_sum_kernel, out_shape=(jax.ShapeDtypeStruct(block,...  45.8 us
    pallas_call x1, Pallas kernels, feed_forward(): pl.pallas_call(ffn_kernel, out_shape=(jax.ShapeDtypeStruct((2 * BLK, D),...  34.9 us
    pallas_call x1, Pallas kernels, pairs_sum(): pl.pallas_call(pairs_sum_kernel, out_shape=(jax.ShapeDtypeStruct(block, j...  33.9 us
    pallas_call x1, Pallas kernels, second_gather(): pl.pallas_call(second_gather_kernel, out_shape=(jax.ShapeDtypeStruct((4,...  33.8 us
    pallas_call x1, Pallas kernels, attend_forward(): pl.pallas_call(forward_kernel, out_shape=(jax.ShapeDtypeStruct((2, KV_HEA...  28 us
    pallas_call x1, Pallas kernels, attend_backward(): pl.pallas_call(backward_kernel, out_shape=(jax.ShapeDtypeStruct((2, KV_HE...  26.3 us
    pallas_call x1, Pallas kernels, first_gather(): pl.pallas_call(first_gather_kernel, out_shape=(jax.ShapeDtypeStruct((2, 4...  20 us
    unnamed x72, local copies, waits for them, and re-layouts  8.69 us
  transfers between devices with their start and end apart: 4, of which 0 were waited for; matrix products, arithmetic and copies ran while one was open for 16% of the time, Pallas kernels for 42%

profile of v3, /device:TPU:0, one launch (start us, length us, event | category | flops | bytes accessed | tf_op | source)
XLA Modules:
  0.0 305.5 jit_solution(17962372982026849702)
XLA Ops:
  15.4 20.0 %shard_map.186 = (bf16[2,4,240,320]{3,2,1,0:T(8,128)(2,1)}, bf16[4,32,128]{2,1,0:T(8,128)(2,1)}) custom-call(bf16[2,240,320]{2,1,0:T(8,128)(2,1)} %pad_maximum_fusion.5.w_ref, bf16[32,128]{1,0:T(8,128)(2,1)} %pad_bitcast_fusion.gain_ref), custom_call_target="tpu_custom_call" | custom-call | bytes 60000000 | tf_op jit(solution)/shard_map/pallas_call | solution.py:669
  35.4 1.5 fusion.66
  42.7 33.8 %shard_map.187 = (bf16[4,4,2,128,640]{4,3,2,1,0:T(8,128)(2,1)}, bf16[2,4,240,480]{3,2,1,0:T(8,128)(2,1)}, bf16[4,80,960]{2,1,0:T(8,128)(2,1)}) custom-call(bf16[128,640]{1,0:T(8,128)(2,1)} %copy.151.kv_ref, bf16[2,240,480]{2,1,0:T(8,128)(2,1)} %pad_maximum_fusion.3.o_ref, bf16[80,960]{1,0:T(8,128)(2,1)} %copy.198.down_ref), custom_call_target="tpu_custom_call" | custom-call | bytes 100000000 | tf_op jit(solution)/shard_map/pallas_call | solution.py:685
  76.4 1.7 fusion.65
  82.8 28.0 %shard_map.188 = (f32[2,5,64,256]{3,2,1,0:T(8,128)S(1)}, f32[2,5,1,256]{3,2,1,0:T(1,128)S(1)}) custom-call(s32[64]{0:T(128)S(1)} %copy-done.2, s32[2]{0:T(128)S(1)} %get-tuple-element.95.mine_ref, bf16[2,5,256,128]{3,2,1,0:T(8,128)(2,1)S(1)} %pad.32.q_ref, bf16[64,64,640]{2,1,0:T(8,128)(2,1)} %bitcast.203), custom_call_target="tpu_custom_call" | custom-call | flops 10000000000 | bytes 8000000 | tf_op jit(solution)/shard_map/pallas_call | solution.py:201
  116.0 2.1 multiply_reduce_fusion.2
  118.9 34.9 %shard_map.189 = (f32[128,960]{1,0:T(8,128)}, bf16[4,2,128,960]{3,2,1,0:T(8,128)(2,1)}, bf16[4,4,240,240]{3,2,1,0:T(8,128)(2,1)}) custom-call(bf16[128,960]{1,0:T(8,128)(2,1)} %multiply_convert_fusion.h_ref, bf16[4,2,960,128]{3,2,1,0:T(8,128)(2,1)} %bitcast.205, bf16[2,960,320]{2,1,0:T(8,128)(2,1)} %all-gather.8.cloned.1.call-done.gate_up_ref, ...), custom_call_target="tpu_custom_call" | custom-call | flops 6000000000 | bytes 12000000 | tf_op jit(solution)/shard_map/pallas_call | solution.py:428
  153.8 1.6 multiply_reduce_fusion
  155.5 2.0 fusion.63
  158.3 2.2 convolution_convert_fusion
  162.0 26.3 %shard_map.190 = (f32[2,5,64,256]{3,2,1,0:T(8,128)S(1)}, bf16[2,4,4,128,640]{4,3,2,1,0:T(8,128)(2,1)}) custom-call(s32[64]{0:T(128)S(1)} %copy-done.2, s32[2]{0:T(128)S(1)} %get-tuple-element.95.mine_ref, bf16[2,5,256,128]{3,2,1,0:T(8,128)(2,1)S(1)} %pad.32.q_ref, bf16[2,5,256,128]{3,2,1,0:T(8,128)(2,1)S(1)} %pad.33.do_ref, ...), custom_call_target="tpu_custom_call" | custom-call | flops 20000000000 | bytes 12000000 | tf_op jit(solution)/shard_map/pallas_call | solution.py:228
  188.3 33.9 %shard_map.191 = (f32[128,640]{1,0:T(8,128)}, bf16[4,240,240]{2,1,0:T(8,128)(2,1)}) custom-call(bf16[2,4,4,128,640]{4,3,2,1,0:T(8,128)(2,1)} %get-tuple-element.39.parts, bf16[4,4,240,240]{3,2,1,0:T(8,128)(2,1)} %get-tuple-element.40.ffn), custom_call_target="tpu_custom_call" | custom-call | tf_op jit(solution)/shard_map/pallas_call | solution.py:882
  224.3 1.3 copy.160
  225.6 2.0 copy.161
  230.5 1.3 fusion.64
  234.1 1.4 fusion.38
  235.5 1.3 fusion.33
  237.3 1.5 fusion.32
  239.8 1.9 pad_maximum_fusion.2.right_ref
  241.7 1.9 pad_maximum_fusion.1.left_ref
  243.6 45.8 %shard_map.192 = (f32[96,240]{1,0:T(8,128)}, bf16[240,240]{1,0:T(8,128)(2,1)}, bf16[4,2,80,240]{3,2,1,0:T(8,128)(2,1)}) custom-call(bf16[2,4,4,96,288]{4,3,2,1,0:T(8,128)(2,1)} %pad_maximum_fusion.1.left_ref, bf16[288,1024]{1,0:T(8,128)(2,1)} %pad_maximum_fusion.2.right_ref, bf16[4,240,240]{2,1,0:T(8,128)(2,1)} %get-tuple-element.42.ffn_ref), custom_call_target="tpu_custom_call" | custom-call | tf_op jit(solution)/shard_map/pallas_call | solution.py:973
  292.9 1.2 slice_bitcast_fusion.5
  294.1 1.4 fusion.71
  295.5 1.4 fusion.72
  (182 shorter events, 40.4 us)
Async XLA Ops:
  7.2 108.8 %all-gather.4.cloned.1.call-start = ((), (), s32[]{:S(2)}) async-start(), calls=%async_computation.1 | async-start | bytes 2457600 | tf_op jit(solution)/shard_map/all_gather | solution.py:1034
  7.9 111.0 %all-gather.8.cloned.1.call-start = ((), (), s32[]{:S(2)}) async-start(), calls=%async_computation.3 | async-start | bytes 1843200 | tf_op jit(solution)/shard_map/all_gather | solution.py:1033
  9.8 2.6 copy-start.21
  10.6 2.0 copy-start.22
  10.6 3.1 %copy-start.24 = (bf16[480]{0:T(512)(128)(2,1)S(1)}, bf16[480]{0:T(512)(128)(2,1)}, u32[]{:S(2)}) copy-start(bf16[480]{0:T(512)(128)(2,1)} %param.14) | copy-start | bytes 2884
  11.6 107.3 %all-gather.6.cloned.1.call-start = ((), (), s32[]{:S(2)}) async-start(), calls=%async_computation.2 | async-start | bytes 2211840 | tf_op jit(solution)/shard_map/all_gather | solution.py:1035
  12.4 280.5 %reduce-scatter.2.cloned.1.call-start = ((), (), s32[]{:S(2)}) async-start(), calls=%async_computation.4 | async-start | bytes 2359296 | tf_op jit(solution)/shard_map/reduce_scatter | solution.py:1069
  14.6 22.3 %copy-start.20 = (bf16[1,128,960]{1,2,0:T(8,128)(2,1)S(1)}, bf16[1,128,960]{1,2,0:T(8,128)(2,1)}, u32[]{:S(2)}) copy-start(bf16[1,128,960]{1,2,0:T(8,128)(2,1)} %param.11) | copy-start | bytes 737284
  35.4 1.7 copy-start.23
  36.9 1.4 copy-start.7
  36.9 1.4 copy-start.9
  37.1 1.3 copy-start.2
  37.8 1.9 copy-start.19
  76.4 3.2 %copy-start.16 = (bf16[1,128,960]{1,2,0:T(8,128)(2,1)S(1)}, bf16[1,128,960]{1,2,0:T(8,128)(2,1)}, u32[]{:S(2)}) copy-start(bf16[1,128,960]{1,2,0:T(8,128)(2,1)} %param.12) | copy-start | bytes 737284
  78.2 2.3 copy-start.5
  227.6 1.4 copy-start.18
  231.8 1.4 copy-start.10
  231.8 1.9 copy-start.8
  231.8 2.3 copy-start.6
  233.2 2.2 copy-start.4
  233.3 2.2 copy-start.15
  237.3 4.4 %copy-start.11 = (bf16[4,4,1,96,288]{4,3,0,1,2:T(8,128)(2,1)S(1)}, bf16[4,4,1,96,288]{4,3,0,1,2:T(8,128)(2,1)}, u32[]{:S(2)}) copy-start(bf16[4,4,1,96,288]{4,3,0,1,2:T(8,128)(2,1)} %copy.208) | copy-start | bytes 2654212
  238.9 2.9 copy-start.12
  243.6 55.1 %copy-start.1 = (bf16[240,2560]{1,0:T(8,128)(2,1)S(1)}, bf16[240,2560]{1,0:T(8,128)(2,1)}, u32[]{:S(2)}) copy-start(bf16[240,2560]{1,0:T(8,128)(2,1)} %param.20) | copy-start | bytes 3686404
  (6 other events, 6.6 us)
Sparse Core Ops, SparseCore 0:
  9.7 34.6 all-gather.3
  46.0 30.4 all-gather.7
  78.2 24.7 all-gather.5
  223.5 32.0 reduce-scatter.1
